TPU v7x, 128 devices: a whole 4x4x4 slice. The times are simulated.
128 devices in a mesh: dp: 16 (over x, y), seq: 8 (over z, core).
Axes of the slice: x: 4, y: 4, z: 4, core: 2. Of those that a mesh axis runs over, the one named last changes fastest.
Arguments:
- queries: bfloat16 [16, 8, 384, 1024], P('dp', 'seq'), may hold values from -6 to 6
- keys: bfloat16 [16, 8, 384, 1024], P('dp', 'seq'), may hold values from -6 to 6
- values: bfloat16 [16, 8, 384, 1024], P('dp', 'seq'), may hold values from -6 to 6
- gates: bfloat16 [16, 8, 384, 1024], P('dp', 'seq'), may hold values from -6 to 6
- attended: bfloat16 [16, 8, 384, 1024], P('dp', 'seq')
- out_grad: bfloat16 [16, 8, 384, 1024], P('dp', 'seq'), may hold values from -6 to 6
- plan: int32 [16, 8, 16], P(None, 'seq'), may hold values from 1 to 24, 256 in all within a row
- hist_len: int32 [16], P('dp'), may hold values from 512 to 2048, as said below
- block_mask: int32 [16, 16, 16], P('dp'), may hold values 0 or 1
Outputs:
- query_grad: bfloat16 [16, 8, 384, 1024], P('dp', 'seq')
- key_grad: bfloat16 [16, 8, 384, 1024], P('dp', 'seq')
- value_grad: bfloat16 [16, 8, 384, 1024], P('dp', 'seq')
- gate_grad: bfloat16 [16, 8, 384, 1024], P('dp', 'seq')
Inputs may be any that keep to these rules, and one draw needn't show every extreme that they name: For every history g and piece s, plan[g, s, :] sums to 256; some entry of each such row equals 24. `hist_len`: some history has exactly 2048 events.
All inputs are finite; a program needn't handle non-finite values. No bound on the sum of `block_mask` on one device may be relied on, other than what follows from the above.
Results may differ from a plain program's by a relative error of at most 0.0058.
Values may be sent and summed in bfloat16 or wider, within the bound.
A program may use at most 128 MiB of HBM per device.

v0:
```python
import jax
import jax.numpy as jnp
from jax import lax
from jax.sharding import PartitionSpec as P

HEADS = 8
ROWS = 256
BLOCK = 128


def layer_norm(inputs):
    center = inputs - jnp.mean(inputs, axis=-1, keepdims=True)
    spread = jnp.mean(center * center, axis=-1, keepdims=True)
    return center * lax.rsqrt(spread + 1e-05)


def flatten(array):
    return array.reshape(array.shape[2], array.shape[3])


def cut_rows(array, offset, extent, head_count):
    return array[offset : offset + extent].reshape(extent, head_count, -1)


def pair_terms(query_rows, grad_rows, key_rows, value_rows, live_weight):
    scale_qk = query_rows.shape[2] ** (-0.5)
    scores = (
        jnp.einsum("thd,shd->hts", query_rows, key_rows, preferred_element_type=jnp.float32)
        * scale_qk
    )
    sigmoid = jax.nn.sigmoid(scores)
    weight = (scores * sigmoid * live_weight[None]).astype(jnp.bfloat16)
    products = jnp.einsum("thd,shd->hts", grad_rows, value_rows, preferred_element_type=jnp.float32)
    score_grad = (
        products * (sigmoid * (1.0 + scores * (1.0 - sigmoid))) * live_weight[None]
    ).astype(jnp.bfloat16)
    query_part = (
        jnp.einsum("hts,shd->thd", score_grad, key_rows, preferred_element_type=jnp.float32)
        * scale_qk
    )
    key_part = (
        jnp.einsum("hts,thd->shd", score_grad, query_rows, preferred_element_type=jnp.float32)
        * scale_qk
    )
    value_part = jnp.einsum("hts,thd->shd", weight, grad_rows, preferred_element_type=jnp.float32)
    return (query_part, key_part, value_part)


def local(queries, keys, values, gates, attended, out_grad, plan, hist_len, block_mask):
    group_count = lax.axis_size("dp")
    capacity = queries.shape[2]
    model_width = queries.shape[3]
    slot_count = capacity // group_count
    row_count = ROWS
    head_count = HEADS
    head_size = model_width // head_count
    dp_index = lax.axis_index("dp")
    seq_index = lax.axis_index("seq")
    group_ids = jnp.arange(group_count, dtype=jnp.int32)
    slot_ids = jnp.arange(slot_count, dtype=jnp.int32)
    row_ids = jnp.arange(row_count, dtype=jnp.int32)
    my_plan = plan[:, 0, :]
    incoming = jnp.sum(jnp.where(group_ids[None, :] == dp_index, my_plan, 0), axis=1)
    valid = (slot_ids[None, :] < incoming[:, None]).reshape(capacity)
    normed, pullback = jax.vjp(layer_norm, flatten(attended).astype(jnp.float32))
    cotangent = flatten(out_grad).astype(jnp.float32) * flatten(gates).astype(jnp.float32)
    attn_grad = pullback(cotangent)[0].astype(jnp.bfloat16)
    gate_grad = jnp.where(
        valid[:, None], flatten(out_grad).astype(jnp.float32) * normed, 0.0
    ).astype(jnp.bfloat16)
    shape_slots = (group_count, slot_count, model_width)
    received = (
        lax.all_to_all(
            flatten(queries).reshape(shape_slots), "dp", split_axis=0, concat_axis=0, tiled=True
        ),
        lax.all_to_all(
            flatten(keys).reshape(shape_slots), "dp", split_axis=0, concat_axis=0, tiled=True
        ),
        lax.all_to_all(
            flatten(values).reshape(shape_slots), "dp", split_axis=0, concat_axis=0, tiled=True
        ),
        lax.all_to_all(
            attn_grad.reshape(shape_slots), "dp", split_axis=0, concat_axis=0, tiled=True
        ),
    )
    own_counts = jnp.sum(jnp.where(group_ids[:, None] == dp_index, my_plan, 0), axis=0)
    cum_incl = jnp.cumsum(own_counts)
    cum_excl = cum_incl - own_counts
    dest = jnp.sum((cum_incl[None, :] <= row_ids[:, None]).astype(jnp.int32), axis=1)
    begin = jnp.sum(jnp.where(group_ids[None, :] == dest[:, None], cum_excl[None, :], 0), axis=1)
    flat_index = dest * slot_count + row_ids - begin
    history = []
    for array in received:
        history.append(
            jnp.take(array.reshape(group_count * slot_count, model_width), flat_index, axis=0)
        )
    length = hist_len[0]
    pattern = block_mask[0].astype(jnp.float32)
    block_total = pattern.shape[0]
    inverse = 1.0 / jnp.sqrt(length.astype(jnp.float32))
    block_ids = jnp.arange(block_total, dtype=jnp.int32)

    def live_mask(query_pos, key_pos):
        query_block = query_pos // BLOCK
        key_block = key_pos // BLOCK
        onehot_query = (query_block[:, None] == block_ids[None, :]).astype(jnp.float32)
        onehot_key = (key_block[:, None] == block_ids[None, :]).astype(jnp.float32)
        blocks = jnp.dot(
            jnp.dot(onehot_query, pattern, precision=lax.Precision.HIGHEST),
            onehot_key.T,
            precision=lax.Precision.HIGHEST,
        )
        keep = (
            (key_pos[None, :] <= query_pos[:, None])
            & (query_pos[:, None] < length)
            & (key_pos[None, :] < length)
        )
        keep = keep & ((blocks > 0.5) | (query_block[:, None] == key_block[None, :]))
        return keep.astype(jnp.float32) * inverse

    own_pos = seq_index * row_count + row_ids
    own_query = history[0].reshape(row_count, head_count, head_size)
    own_key = history[1].reshape(row_count, head_count, head_size)
    own_value = history[2].reshape(row_count, head_count, head_size)
    own_grad = history[3].reshape(row_count, head_count, head_size)
    zeros = jnp.zeros((row_count, head_count, head_size), jnp.float32)
    anchor = jnp.int32(0)
    shard_query = lax.all_gather(history[0], "seq", axis=0, tiled=True)
    shard_key = lax.all_gather(history[1], "seq", axis=0, tiled=True)
    shard_value = lax.all_gather(history[2], "seq", axis=0, tiled=True)
    shard_grad = lax.all_gather(history[3], "seq", axis=0, tiled=True)
    total = shard_query.shape[0]
    query_sum = zeros
    key_sum = zeros
    value_sum = zeros
    for offset in range(0, total, 1024):
        extent = min(1024, total - offset)
        positions = anchor + offset + jnp.arange(extent, dtype=jnp.int32)
        part_query = cut_rows(shard_query, offset, extent, head_count)
        part_key = cut_rows(shard_key, offset, extent, head_count)
        part_value = cut_rows(shard_value, offset, extent, head_count)
        part_grad = cut_rows(shard_grad, offset, extent, head_count)
        earlier = pair_terms(
            own_query, own_grad, part_key, part_value, live_mask(own_pos, positions)
        )
        later = pair_terms(part_query, part_grad, own_key, own_value, live_mask(positions, own_pos))
        query_sum = query_sum + earlier[0]
        key_sum = key_sum + later[1]
        value_sum = value_sum + later[2]
    sums = (query_sum, key_sum, value_sum)
    grads = [array.astype(jnp.bfloat16).reshape(row_count, model_width) for array in sums]
    row_index = jnp.minimum(cum_excl[:, None] + slot_ids[None, :], row_count - 1).reshape(-1)
    keep_slots = (slot_ids[None, :] < own_counts[:, None]).reshape(-1)

    def pack(array):
        picked = jnp.take(array, row_index, axis=0)
        return jnp.where(keep_slots[:, None], picked, 0.0).reshape(shape_slots)

    returned = (
        lax.all_to_all(pack(grads[0]), "dp", split_axis=0, concat_axis=0, tiled=True),
        lax.all_to_all(pack(grads[1]), "dp", split_axis=0, concat_axis=0, tiled=True),
        lax.all_to_all(pack(grads[2]), "dp", split_axis=0, concat_axis=0, tiled=True),
    )
    out_shape = (1, 1, capacity, model_width)
    return (
        returned[0].reshape(out_shape),
        returned[1].reshape(out_shape),
        returned[2].reshape(out_shape),
        gate_grad.reshape(out_shape),
    )


def solution(mesh):
    in_specs = (
        P("dp", "seq", None, None),
        P("dp", "seq", None, None),
        P("dp", "seq", None, None),
        P("dp", "seq", None, None),
        P("dp", "seq", None, None),
        P("dp", "seq", None, None),
        P(None, "seq", None),
        P("dp"),
        P("dp", None, None),
    )
    out_specs = (
        P("dp", "seq", None, None),
        P("dp", "seq", None, None),
        P("dp", "seq", None, None),
        P("dp", "seq", None, None),
    )
    return jax.shard_map(local, mesh=mesh, in_specs=in_specs, out_specs=out_specs, check_vma=False)
```

profile of v0, /device:TPU:0, one launch (start us, length us, event | category | flops | bytes accessed | tf_op | source)
XLA Modules:
  0.0 369.2 jit_solution(3230899232040963151)
XLA Ops:
  8.8 2.2 multiply_reduce_fusion
  11.1 2.3 fusion.18
  13.9 1.9 fusion.15
  15.9 1.9 fusion.17
  17.8 21.0 %all_to_all.35 = bf16[16,24,1024]{2,1,0:T(8,128)(2,1)S(1)} all-to-all(bf16[16,24,1024]{2,1,0:T(8,128)(2,1)S(1)} %fusion.17), channel_id=1, replica_groups=mesh['dp'=16,'seq'=8] {'dp'}, dimensions={0} | all-to-all | bytes 1572864 | tf_op jit(solution)/shard_map/all_to_all | solution.py:82
  38.8 16.4 %all_to_all.36 = bf16[16,24,1024]{2,1,0:T(8,128)(2,1)S(1)} all-to-all(bf16[16,24,1024]{2,1,0:T(8,128)(2,1)S(1)} %bitcast.158), channel_id=1, replica_groups=mesh['dp'=16,'seq'=8] {'dp'}, dimensions={0} | all-to-all | bytes 1572864 | tf_op jit(solution)/shard_map/all_to_all | solution.py:76
  55.2 15.4 %all_to_all.37 = bf16[16,24,1024]{2,1,0:T(8,128)(2,1)S(1)} all-to-all(bf16[16,24,1024]{2,1,0:T(8,128)(2,1)} %bitcast.159), channel_id=1, replica_groups=mesh['dp'=16,'seq'=8] {'dp'}, dimensions={0} | all-to-all | bytes 1572864 | tf_op jit(solution)/shard_map/all_to_all | solution.py:79
  70.6 3.6 all-to-all-start.3
  74.7 2.0 gather_fusion.1
  76.7 2.0 gather_fusion
  79.8 5.9 %all-to-all-done.3 = bf16[16,24,1024]{2,1,0:T(8,128)(2,1)S(1)} async-done(((bf16[16,24,1024]{2,1,0:T(8,128)(2,1)}), bf16[16,24,1024]{2,1,0:T(8,128)(2,1)S(1)}, u32[]{:S(2)}, u32[]{:S(2)}) %all-to-all-start.3) | async-done | bytes 786464 | tf_op jit(solution)/shard_map/all_to_all | solution.py:73
  87.0 1.6 broadcast_select_fusion
  92.9 2.1 fusion.30
  95.0 2.1 fusion.33
  97.0 2.0 fusion.36
  99.0 2.1 fusion.39
  101.1 18.8 %all-gather.7.cloned.1.call-done = bf16[2048,1024]{1,0:T(8,128)(2,1)} async-done(((bf16[256,1024]{1,0:T(8,128)(2,1)}), bf16[2048,1024]{1,0:T(8,128)(2,1)}) %all-gather.7.cloned.1.call-update) | async-done | bytes 4194320 | tf_op jit(solution)/shard_map/all_gather | solution.py:130
  119.9 4.0 %fusion.111 = (bf16[1024,1024]{1,0:T(8,128)(2,1)}, bf16[1024,1024]{1,0:T(8,128)(2,1)S(1)}) fusion(bf16[2048,1024]{1,0:T(8,128)(2,1)} %all-gather.7.cloned.1.call-done), kind=kLoop, calls=%fused_computation.176 | loop fusion | bytes 8388608 | tf_op jit(solution)/shard_map/slice | solution.py:22
  124.0 2.8 copy.69
  126.8 27.6 %all-gather.9.cloned.1.call-done = bf16[2048,1024]{1,0:T(8,128)(2,1)} async-done(((bf16[256,1024]{1,0:T(8,128)(2,1)}), bf16[2048,1024]{1,0:T(8,128)(2,1)}) %all-gather.9.cloned.1.call-update) | async-done | bytes 4194320 | tf_op jit(solution)/shard_map/all_gather | solution.py:128
  154.4 4.0 %fusion.110 = (bf16[1024,1024]{1,0:T(8,128)(2,1)S(1)}, bf16[1024,1024]{1,0:T(8,128)(2,1)}) fusion(bf16[2048,1024]{1,0:T(8,128)(2,1)} %all-gather.9.cloned.1.call-done), kind=kLoop, calls=%fused_computation.175 | loop fusion | bytes 8388608 | tf_op jit(solution)/shard_map/slice | solution.py:22
  158.4 3.9 %copy.81 = bf16[1024,1024]{0,1:T(8,128)(2,1)} copy(bf16[1024,1024]{1,0:T(8,128)(2,1)} %get-tuple-element.15) | data formatting | bytes 4194304 | tf_op jit(solution)/shard_map/slice | solution.py:22
  162.4 26.5 %all-gather.11.cloned.1.call-done = bf16[2048,1024]{1,0:T(8,128)(2,1)} async-done(((bf16[256,1024]{1,0:T(8,128)(2,1)}), bf16[2048,1024]{1,0:T(8,128)(2,1)}) %all-gather.11.cloned.1.call-update) | async-done | bytes 4194320 | tf_op jit(solution)/shard_map/all_gather | solution.py:131
  188.9 4.7 %fusion.109 = (bf16[1024,1024]{1,0:T(8,128)(2,1)}, bf16[1024,1024]{1,0:T(8,128)(2,1)}) fusion(bf16[2048,1024]{1,0:T(8,128)(2,1)} %all-gather.11.cloned.1.call-done), kind=kLoop, calls=%fused_computation.174 | loop fusion | bytes 8388608 | tf_op jit(solution)/shard_map/slice | solution.py:22
  193.6 4.0 %copy.82 = bf16[1024,1024]{0,1:T(8,128)(2,1)} copy(bf16[1024,1024]{1,0:T(8,128)(2,1)} %get-tuple-element.13) | data formatting | bytes 4194304 | tf_op jit(solution)/shard_map/slice | solution.py:22
  197.6 6.3 %fusion.58 = f32[8,256,1024]{2,1,0:T(8,128)} fusion(bf16[1024,8,128]{0,2,1:T(8,128)(2,1)} %bitcast.140, bf16[256,1024]{1,0:T(8,128)(2,1)S(1)} %copy-done.5), kind=kOutput, calls=%fused_computation.83 | convolution fusion | flops 536870912 | bytes 11010048 | tf_op jit(solution)/shard_map/thd,shd->hts/dot_general | solution.py:33
  205.3 3.2 copy-done.1
  208.5 4.1 %fusion = f32[8,128,256]{2,1,0:T(8,128)} fusion(bf16[1024,8,128]{0,2,1:T(8,128)(2,1)S(1)} %bitcast.157, f32[8,1024,256]{2,1,0:T(8,128)S(1)} %fusion.46, f32[1024,256]{1,0:T(8,128)S(1)} %copy-done.16), kind=kOutput, calls=%fused_computation.15 | convolution fusion | flops 551550976 | bytes 12582912 | tf_op jit(solution)/shard_map/hts,thd->shd/dot_general | solution.py:45
  212.6 10.7 %fusion.4 = f32[8,128,256]{2,1,0:T(8,128)} fusion(bf16[1024,8,128]{0,2,1:T(8,128)(2,1)} %bitcast.141, f32[8,1024,256]{2,1,0:T(8,128)} %copy-done.1, f32[1024,256]{1,0:T(8,128)} %fusion.36, bf16[1024,8,128]{0,2,1:T(8,128)(2,1)} %bitcast.156, bf16[256,1024]{1,0:T(8,128)(2,1)} %get-tuple-element.32), kind=kOutput, calls=%fused_computation.19 | convolution fusion | flops 1096810496 | bytes 15204352 | tf_op jit(solution)/shard_map/hts,thd->shd/dot_general | solution.py:42
  223.3 4.8 %fusion.112 = (bf16[1024,1024]{1,0:T(8,128)(2,1)}, bf16[1024,1024]{1,0:T(8,128)(2,1)}) fusion(bf16[2048,1024]{1,0:T(8,128)(2,1)} %all-gather.5.cloned.1.call-done), kind=kLoop, calls=%fused_computation.177 | loop fusion | bytes 8388608 | tf_op jit(solution)/shard_map/slice | solution.py:22
  228.2 4.0 %copy.68 = bf16[1024,1024]{0,1:T(8,128)(2,1)} copy(bf16[1024,1024]{1,0:T(8,128)(2,1)} %get-tuple-element.19) | data formatting | bytes 4194304 | tf_op jit(solution)/shard_map/slice | solution.py:22
  232.1 4.3 %copy.75 = bf16[1024,1024]{0,1:T(8,128)(2,1)} copy(bf16[1024,1024]{1,0:T(8,128)(2,1)} %get-tuple-element.16) | data formatting | bytes 4194304 | tf_op jit(solution)/shard_map/slice | solution.py:22
  236.5 6.1 %fusion.56 = f32[8,256,1024]{2,1,0:T(8,128)} fusion(bf16[1024,8,128]{0,2,1:T(8,128)(2,1)} %bitcast.145, bf16[256,1024]{1,0:T(8,128)(2,1)S(1)} %copy-done.5), kind=kOutput, calls=%fused_computation.81 | convolution fusion | flops 536870912 | bytes 11010048 | tf_op jit(solution)/shard_map/thd,shd->hts/dot_general | solution.py:33
  242.5 4.0 %copy.74 = bf16[1024,1024]{0,1:T(8,128)(2,1)} copy(bf16[1024,1024]{1,0:T(8,128)(2,1)} %get-tuple-element.18) | data formatting | bytes 4194304 | tf_op jit(solution)/shard_map/slice | solution.py:22
  246.5 10.8 %fusion.2 = f32[8,128,256]{2,1,0:T(8,128)} fusion(bf16[1024,8,128]{0,2,1:T(8,128)(2,1)} %bitcast.154, f32[8,256,1024]{2,1,0:T(8,128)} %fusion.58, f32[256,1024]{1,0:T(8,128)} %fusion.30, bf16[256,1024]{1,0:T(8,128)(2,1)S(1)} %copy-done.11), kind=kOutput, calls=%fused_computation.17 | convolution fusion | flops 1096810496 | bytes 13107200 | tf_op jit(solution)/shard_map/hts,shd->thd/dot_general | solution.py:38
  257.3 10.8 %fusion.26 = bf16[8,128,256]{2,1,0:T(8,128)(2,1)} fusion(f32[8,128,256]{2,1,0:T(8,128)} %fusion.2, bf16[1024,8,128]{0,2,1:T(8,128)(2,1)} %bitcast.155, f32[8,256,1024]{2,1,0:T(8,128)} %fusion.56, f32[256,1024]{1,0:T(8,128)} %fusion.33, bf16[256,1024]{1,0:T(8,128)(2,1)S(1)} %copy-done.11), kind=kOutput, calls=%fused_computation.46 | convolution fusion | flops 1097596928 | bytes 13631488 | tf_op jit(solution)/shard_map/hts,shd->thd/dot_general | solution.py:38
  269.4 2.7 copy.87
  272.1 6.3 %fusion.44 = f32[8,1024,256]{2,1,0:T(8,128)} fusion(bf16[1024,8,128]{0,2,1:T(8,128)(2,1)} %bitcast.143, bf16[256,1024]{1,0:T(8,128)(2,1)S(1)} %copy-done.4), kind=kOutput, calls=%fused_computation.73 | convolution fusion | flops 536870912 | bytes 11010048 | tf_op jit(solution)/shard_map/thd,shd->hts/dot_general | solution.py:28
  278.4 2.6 copy.88
  281.0 9.7 %fusion.27 = bf16[8,128,256]{2,1,0:T(8,128)(2,1)S(1)} fusion(f32[8,128,256]{2,1,0:T(8,128)} %fusion.4, bf16[1024,8,128]{0,2,1:T(8,128)(2,1)} %bitcast.144, f32[8,1024,256]{2,1,0:T(8,128)} %fusion.44, f32[1024,256]{1,0:T(8,128)} %fusion.39, bf16[1024,8,128]{0,2,1:T(8,128)(2,1)} %bitcast.152, bf16[256,1024]{1,0:T(8,128)(2,1)S(1)} %copy-done.10), kind=kOutput, calls=%fused_computation.47 | convolution fusion | flops 1097596928 | bytes 15728640 | tf_op jit(solution)/shard_map/hts,thd->shd/dot_general | solution.py:42
  290.9 2.1 gather_fusion.4
  293.0 2.1 gather_fusion.5
  295.1 7.2 %fusion.25 = bf16[8,128,256]{2,1,0:T(8,128)(2,1)S(1)} fusion(f32[8,128,256]{2,1,0:T(8,128)} %fusion, bf16[1024,8,128]{0,2,1:T(8,128)(2,1)} %bitcast.153, f32[8,1024,256]{2,1,0:T(8,128)} %fusion.44, f32[1024,256]{1,0:T(8,128)} %fusion.39), kind=kOutput, calls=%fused_computation.45 | convolution fusion | flops 552075264 | bytes 13107200 | tf_op jit(solution)/shard_map/hts,thd->shd/dot_general | solution.py:45
  302.5 2.1 gather_fusion.6
  305.9 21.1 %all_to_all.38 = bf16[16,24,1024]{2,1,0:T(8,128)(2,1)S(1)} all-to-all(bf16[16,24,1024]{2,1,0:T(8,128)(2,1)S(1)} %bitcast.148), channel_id=1, replica_groups=mesh['dp'=16,'seq'=8] {'dp'}, dimensions={0} | all-to-all | bytes 1572864 | tf_op jit(solution)/shard_map/all_to_all | solution.py:160
  327.0 16.8 %all_to_all.39 = bf16[16,24,1024]{2,1,0:T(8,128)(2,1)S(1)} all-to-all(bf16[16,24,1024]{2,1,0:T(8,128)(2,1)S(1)} %bitcast.147), channel_id=1, replica_groups=mesh['dp'=16,'seq'=8] {'dp'}, dimensions={0} | all-to-all | bytes 1572864 | tf_op jit(solution)/shard_map/all_to_all | solution.py:161
  343.8 3.6 all-to-all-start.6
  347.5 12.4 %all-to-all-done.6 = bf16[16,24,1024]{2,1,0:T(8,128)(2,1)S(1)} async-done(((bf16[16,24,1024]{2,1,0:T(8,128)(2,1)}), bf16[16,24,1024]{2,1,0:T(8,128)(2,1)S(1)}, u32[]{:S(2)}, u32[]{:S(2)}) %all-to-all-start.6) | async-done | bytes 786464 | tf_op jit(solution)/shard_map/all_to_all | solution.py:162
  (87 shorter events, 15.4 us)
Async XLA Ops:
  7.2 6.6 %copy-start = (bf16[1,1,384,1024]{3,2,1,0:T(8,128)(2,1)S(1)}, bf16[1,1,384,1024]{3,2,1,0:T(8,128)(2,1)}, u32[]{:S(2)}) copy-start(bf16[1,1,384,1024]{3,2,1,0:T(8,128)(2,1)} %param.17) | copy-start | bytes 2359300
  7.2 6.6 %copy-start.7 = (bf16[1,1,384,1024]{3,2,1,0:T(8,128)(2,1)S(1)}, bf16[1,1,384,1024]{3,2,1,0:T(8,128)(2,1)}, u32[]{:S(2)}) copy-start(bf16[1,1,384,1024]{3,2,1,0:T(8,128)(2,1)} %param.16) | copy-start | bytes 2359300
  7.2 6.6 %copy-start.6 = (bf16[1,1,384,1024]{3,2,1,0:T(8,128)(2,1)S(1)}, bf16[1,1,384,1024]{3,2,1,0:T(8,128)(2,1)}, u32[]{:S(2)}) copy-start(bf16[1,1,384,1024]{3,2,1,0:T(8,128)(2,1)} %param.18) | copy-start | bytes 2359300
  7.2 6.3 %copy-start.14 = (s32[16,1,16]{2,1,0:T(1,128)S(1)}, s32[16,1,16]{2,1,0:T(1,128)}, u32[]{:S(2)}) copy-start(s32[16,1,16]{2,1,0:T(1,128)} %param.19) | copy-start | bytes 3076
  13.8 25.0 %copy-start.13 = (bf16[1,1,384,1024]{3,2,1,0:T(8,128)(2,1)S(1)}, bf16[1,1,384,1024]{3,2,1,0:T(8,128)(2,1)}, u32[]{:S(2)}) copy-start(bf16[1,1,384,1024]{3,2,1,0:T(8,128)(2,1)} %param.14) | copy-start | bytes 2359300
  70.6 15.1 %all-to-all-start.3 = ((bf16[16,24,1024]{2,1,0:T(8,128)(2,1)}), bf16[16,24,1024]{2,1,0:T(8,128)(2,1)S(1)}, u32[]{:S(2)}, u32[]{:S(2)}) async-start(bf16[16,24,1024]{2,1,0:T(8,128)(2,1)} %bitcast.160), calls=%async_computation.3 | async-start | bytes 1572864 | tf_op jit(solution)/shard_map/all_to_all | solution.py:73
  74.3 45.7 %all-gather.7.cloned.1.call-start = ((), (), s32[]{:S(2)}) async-start(), calls=%async_computation.8 | async-start | bytes 4718592 | tf_op jit(solution)/shard_map/all_gather | solution.py:130
  78.7 8.3 %copy-start.8 = (bf16[256,1024]{1,0:T(8,128)(2,1)S(1)}, bf16[256,1024]{1,0:T(8,128)(2,1)}, u32[]{:S(2)}) copy-start(bf16[256,1024]{1,0:T(8,128)(2,1)} %gather_fusion.1) | copy-start | bytes 1572868
  78.7 8.3 %copy-start.9 = (bf16[256,1024]{1,0:T(8,128)(2,1)S(1)}, bf16[256,1024]{1,0:T(8,128)(2,1)}, u32[]{:S(2)}) copy-start(bf16[256,1024]{1,0:T(8,128)(2,1)} %gather_fusion) | copy-start | bytes 1572868
  86.9 4.7 %copy-start.15 = (s32[1,16,16]{2,1,0:T(8,128)S(1)}, s32[1,16,16]{2,1,0:T(8,128)}, u32[]{:S(2)}) copy-start(s32[1,16,16]{2,1,0:T(8,128)} %param.21) | copy-start | bytes 3076
  88.6 65.8 %all-gather.9.cloned.1.call-start = ((), (), s32[]{:S(2)}) async-start(), calls=%async_computation.9 | async-start | bytes 4718592 | tf_op jit(solution)/shard_map/all_gather | solution.py:128
  89.3 99.5 %all-gather.11.cloned.1.call-start = ((), (), s32[]{:S(2)}) async-start(), calls=%async_computation.10 | async-start | bytes 4718592 | tf_op jit(solution)/shard_map/all_gather | solution.py:131
  90.0 133.3 %all-gather.5.cloned.1.call-start = ((), (), s32[]{:S(2)}) async-start(), calls=%async_computation.7 | async-start | bytes 4718592 | tf_op jit(solution)/shard_map/all_gather | solution.py:129
  193.6 4.0 %copy-start.5 = (bf16[256,1024]{1,0:T(8,128)(2,1)S(1)}, bf16[256,1024]{1,0:T(8,128)(2,1)}, u32[]{:S(2)}) copy-start(bf16[256,1024]{1,0:T(8,128)(2,1)} %get-tuple-element.31) | copy-start | bytes 1572868
  197.6 6.3 %copy-start.3 = (bf16[1024,1024]{0,1:T(8,128)(2,1)S(1)}, bf16[1024,1024]{0,1:T(8,128)(2,1)}, u32[]{:S(2)}) copy-start(bf16[1024,1024]{0,1:T(8,128)(2,1)} %copy.81) | copy-start | bytes 6291460
  197.6 6.3 %copy-start.4 = (bf16[256,1024]{1,0:T(8,128)(2,1)S(1)}, bf16[256,1024]{1,0:T(8,128)(2,1)}, u32[]{:S(2)}) copy-start(bf16[256,1024]{1,0:T(8,128)(2,1)} %get-tuple-element.33) | copy-start | bytes 1572868
  203.9 4.6 %copy-start.12 = (bf16[1024,1024]{0,1:T(8,128)(2,1)S(1)}, bf16[1024,1024]{0,1:T(8,128)(2,1)}, u32[]{:S(2)}) copy-start(bf16[1024,1024]{0,1:T(8,128)(2,1)} %copy.82) | copy-start | bytes 6291460
  203.9 4.6 %copy-start.16 = (f32[1024,256]{1,0:T(8,128)S(1)}, f32[1024,256]{1,0:T(8,128)}, u32[]{:S(2)}) copy-start(f32[1024,256]{1,0:T(8,128)} %fusion.36) | copy-start | bytes 3145732
  205.3 3.2 copy-start.1
  242.5 4.0 %copy-start.11 = (bf16[256,1024]{1,0:T(8,128)(2,1)S(1)}, bf16[256,1024]{1,0:T(8,128)(2,1)}, u32[]{:S(2)}) copy-start(bf16[256,1024]{1,0:T(8,128)(2,1)} %get-tuple-element.30) | copy-start | bytes 1572868
  272.1 6.3 %copy-start.2 = (bf16[1024,1024]{1,0:T(8,128)(2,1)S(1)}, bf16[1024,1024]{1,0:T(8,128)(2,1)}, u32[]{:S(2)}) copy-start(bf16[1024,1024]{1,0:T(8,128)(2,1)} %get-tuple-element.12) | copy-start | bytes 6291460
  278.4 2.7 copy-start.10
  343.8 16.0 %all-to-all-start.6 = ((bf16[16,24,1024]{2,1,0:T(8,128)(2,1)}), bf16[16,24,1024]{2,1,0:T(8,128)(2,1)S(1)}, u32[]{:S(2)}, u32[]{:S(2)}) async-start(bf16[16,24,1024]{2,1,0:T(8,128)(2,1)} %bitcast.33), calls=%async_computation.6 | async-start | bytes 1572864 | tf_op jit(solution)/shard_map/all_to_all | solution.py:162
Sparse Core Ops, SparseCore 0:
  88.7 31.2 all-gather.6
  122.2 32.1 all-gather.8
  156.7 32.1 all-gather.10
  190.4 32.1 all-gather.4
where the time goes:
time: 375 us; the launch traced here: 369 us
  waiting for transfers between devices  92.7 us (25%)
  blocking collectives  90.8 us (24%)
  matrix products  82.7 us (22%)
  local copies, waits for them, and re-layouts  66.8 us (18%)
  between operations  15 us (4%)
  other arithmetic  13.3 us (4%)
  starting transfers between devices  7.89 us (2%)
    slice x12, local copies, waits for them, and re-layouts, cut_rows(): return array[offset:offset + extent].reshape(extent, head_count, -1)  46 us
    all_gather x1, waiting for transfers between devices, local(): shard_query = lax.all_gather(history[0], 'seq', axis=0, tiled=True)  27.6 us
    all_gather x1, waiting for transfers between devices, local(): shard_grad = lax.all_gather(history[3], 'seq', axis=0, tiled=True)  26.5 us
    dot_general x2, matrix products, pair_terms(): jnp.einsum('hts,shd->thd', score_grad, key_rows, preferred_element_type=j...  21.6 us
    all_to_all x1, blocking collectives, local(): lax.all_to_all(pack(grads[0]), 'dp', split_axis=0, concat_axis=0, tiled=T...  21.1 us
    all_to_all x1, blocking collectives, local(): lax.all_to_all(attn_grad.reshape(shape_slots), 'dp', split_axis=0, concat...  21 us
    dot_general x2, matrix products, pair_terms(): jnp.einsum('hts,thd->shd', score_grad, query_rows, preferred_element_type...  20.4 us
    all_gather x1, waiting for transfers between devices, local(): shard_value = lax.all_gather(history[2], 'seq', axis=0, tiled=True)  18.8 us
  transfers between devices with their start and end apart: 6, of which 5 were waited for; matrix products, arithmetic and copies ran while one was open for 17% of the time, Pallas kernels for 0%

commit v1 on v0

v1 whole, which is shorter than its diff:
```python
import jax
import jax.numpy as jnp
from jax import lax
from jax.experimental import pallas as pl
from jax.experimental.pallas import tpu as pltpu
from jax.sharding import PartitionSpec as P

MESH = pl.DeviceIdType.MESH
F32 = jnp.float32
BF16 = jnp.bfloat16

DP = 16
SEQ = 8
SLOT = 24
CAP = 384
WIDTH = 1024
ROWS = 256
DH = 128
LEN = 2048
NBLK = 16
PACK = 2 * SLOT
HALF = 512
QUART = 256
SCALE = DH ** (-0.5)

Q, K, G, V = 0, 1, 2, 3
DV, DK, DQ = 0, 1, 2


def kernel(
    queries,
    keys,
    values,
    gates,
    attended,
    out_grad,
    plan,
    hist_len,
    block_mask,
    query_grad,
    key_grad,
    value_grad,
    gate_grad,
    stage,
    dsend,
    drecv,
    comp,
    hist,
    live,
    wt,
    dt,
    qacc,
    grads,
    gath,
    osend,
    orecv,
    ostage,
    gstage,
    place,
    spread,
    load_sem,
    store_sem,
    dsend_sem,
    drecv_sem,
    ssend_sem,
    srecv_sem,
    gsend_sem,
    grecv_sem,
    osend_sem,
    orecv_sem,
):
    dp = lax.axis_index("dp")
    sq = lax.axis_index("seq")
    row_x, row_y = dp // 4, lax.rem(dp, 4)
    zed, core = sq // 2, lax.rem(sq, 2)

    barrier = pltpu.get_barrier_semaphore()

    def greet_dp(k, carry):
        pl.semaphore_signal(
            barrier, inc=1, device_id=(lax.rem(dp + k, DP), sq), device_id_type=MESH
        )
        return carry

    def greet_seq(k, carry):
        pl.semaphore_signal(
            barrier, inc=1, device_id=(dp, lax.rem(sq + k, SEQ)), device_id_type=MESH
        )
        return carry

    lax.fori_loop(1, DP, greet_dp, 0)
    lax.fori_loop(1, SEQ, greet_seq, 0)

    sources = (queries, keys, attended, gates, out_grad, values)
    loads = [
        pltpu.make_async_copy(src.at[0, 0], stage.at[i], load_sem.at[i])
        for i, src in enumerate(sources)
    ]
    for load in loads:
        load.start()

    def remote(src, dst, send_sem, recv_sem, target):
        return pltpu.make_async_remote_copy(
            src_ref=src,
            dst_ref=dst,
            send_sem=send_sem,
            recv_sem=recv_sem,
            device_id=target,
            device_id_type=MESH,
        )

    def landed(ref, sem):
        remote(ref, ref, sem, sem, (dp, sq)).wait_recv()

    def left(ref, sem):
        remote(ref, ref, sem, sem, (dp, sq)).wait_send()

    def scatter_dp(src, dst, send_sems, recv_sems, chunk):
        def body(k, carry):
            off = k ^ 10
            peer = lax.rem(row_x + off // 4, 4) * 4 + lax.rem(row_y + lax.rem(off, 4), 4)

            @pl.when(k != 10)
            def _():
                remote(
                    src.at[chunk, peer],
                    dst.at[chunk, dp],
                    send_sems.at[chunk],
                    recv_sems.at[chunk],
                    (peer, sq),
                ).start()

            @pl.when(k == 10)
            def _():
                pltpu.make_async_copy(
                    src.at[chunk, dp], dst.at[chunk, dp], recv_sems.at[chunk]
                ).start()

            return carry

        lax.fori_loop(0, DP, body, 0)

    def pack_pair(block, array, pair):
        for half in range(2):
            for side in range(2):
                part = block[side * SLOT : (side + 1) * SLOT]
                at = half * HALF
                message = jnp.concatenate(
                    [part[:, at : at + QUART], part[:, at + QUART : at + HALF]], axis=0
                )
                dsend[2 * array + half, 2 * pair + side] = message.astype(BF16)

    def pack(array, slot):
        loads[slot].wait()

        def body(pair, carry):
            at = pl.multiple_of(pair * PACK, PACK)
            pack_pair(stage[slot, pl.ds(at, PACK), :].astype(F32), array, pair)
            return carry

        lax.fori_loop(0, DP // 2, body, 0)

    def send(array):
        for half in range(2):
            scatter_dp(dsend, drecv, dsend_sem, drecv_sem, 2 * array + half)

    pack(Q, 0)
    pl.semaphore_wait(barrier, DP - 1 + SEQ - 1)
    send(Q)
    pack(K, 1)
    send(K)

    for i in (2, 3, 4):
        loads[i].wait()
    row48 = lax.broadcasted_iota(jnp.int32, (PACK, 1), 0)

    def norm_body(pair, carry):
        at = pl.multiple_of(pair * PACK, PACK)
        inputs = stage[2, pl.ds(at, PACK), :].astype(F32)
        gate = stage[3, pl.ds(at, PACK), :].astype(F32)
        grad = stage[4, pl.ds(at, PACK), :].astype(F32)
        center = inputs - jnp.mean(inputs, axis=-1, keepdims=True)
        spread_ = jnp.mean(center * center, axis=-1, keepdims=True)
        inv = lax.rsqrt(spread_ + 1e-05)
        normed = center * inv
        first = plan[2 * pair, 0, dp]
        second = plan[2 * pair + 1, 0, dp]
        valid = row48 < jnp.where(row48 < SLOT, first, SLOT + second)
        gstage[pl.ds(at, PACK), :] = jnp.where(valid, grad * normed, 0.0).astype(BF16)
        cot = grad * gate
        mean_cot = jnp.mean(cot, axis=-1, keepdims=True)
        mean_dot = jnp.mean(cot * normed, axis=-1, keepdims=True)
        back = inv * (cot - mean_cot - normed * mean_dot)
        pack_pair(jnp.where(valid, back, 0.0), G, pair)
        return carry

    lax.fori_loop(0, DP // 2, norm_body, 0)
    send(G)
    gate_store = pltpu.make_async_copy(gstage, gate_grad.at[0, 0], store_sem.at[0])
    gate_store.start()
    pack(V, 5)
    send(V)

    lane768 = lax.broadcasted_iota(jnp.int32, (1, DP * PACK), 1)
    lane512 = lax.broadcasted_iota(jnp.int32, (1, 2 * ROWS), 1)
    side48 = jnp.where(row48 < SLOT, 0, 1)
    slot48 = row48 - side48 * SLOT

    def target_body(d, carry):
        begin, where_to = carry
        count = plan[dp, 0, d]
        i = lane768 - d * PACK
        side = jnp.where(i < SLOT, 0, 1)
        j = i - side * SLOT
        hit = (i >= 0) & (i < PACK) & (j < count)
        where_to = jnp.where(hit, side * ROWS + begin + j, where_to)
        at = jnp.where(slot48 < count, side48 * ROWS + begin + slot48, -1)
        spread[pl.ds(pl.multiple_of(d * PACK, PACK), PACK), :] = (
            jnp.where(lane512 == at, 1.0, 0.0).astype(BF16)
        )
        return begin + count, where_to

    _, where_to = lax.fori_loop(
        0, DP, target_body, (jnp.int32(0), jnp.full((1, DP * PACK), -1, jnp.int32))
    )

    def place_body(i, carry):
        at = pl.multiple_of(i * 64, 64)
        rows = lax.broadcasted_iota(jnp.int32, (64, 1), 0) + at
        place[pl.ds(at, 64), :] = jnp.where(rows == where_to, 1.0, 0.0).astype(BF16)
        return carry

    lax.fori_loop(0, 2 * ROWS // 64, place_body, 0)

    pattern = block_mask[0].astype(F32)
    block_row = lax.broadcasted_iota(jnp.int32, (NBLK, LEN), 0)
    pos = lax.broadcasted_iota(jnp.int32, (NBLK, LEN), 1)
    onehot = jnp.where(block_row == pos // DH, 1.0, 0.0)
    kept = lax.dot_general(
        pattern, onehot, (((0,), (0,)), ((), ())), preferred_element_type=F32
    )
    length = hist_len[0]
    total = jnp.full((NBLK, LEN), length, jnp.int32).astype(F32)
    inverse = 1.0 / jnp.sqrt(total)
    live[...] = jnp.where(
        ((kept > 0.5) | (onehot > 0.5)) & (pos < length), inverse, 0.0
    )

    def gather_rows(array):
        for half in range(2):
            chunk = 2 * array + half
            landed(drecv.at[chunk], drecv_sem.at[chunk])
            block = drecv[chunk].reshape(DP * PACK, QUART)
            comp[chunk] = jnp.dot(
                place[...], block, preferred_element_type=F32
            ).astype(BF16)
            for to in range(4):
                src = comp.at[
                    chunk, pl.ds(to // 2 * ROWS, ROWS), pl.ds(to % 2 * DH, DH)
                ]
                dst = hist.at[array, sq]
                peer = 2 * to + half

                @pl.when(sq != peer)
                def _():
                    remote(
                        src, dst, ssend_sem.at[array], srecv_sem.at[array], (dp, peer)
                    ).start()

                @pl.when(sq == peer)
                def _():
                    pltpu.make_async_copy(src, dst, srecv_sem.at[array]).start()

    def history(array):
        landed(hist.at[array], srecv_sem.at[array])

    nt = (((1,), (1,)), ((), ()))
    tn = (((0,), (0,)), ((), ()))

    def scores_tile(i, j, diagonal):
        at = pl.multiple_of(j * ROWS, ROWS)
        raw = lax.dot_general(hist[K, i], hist[Q, j], nt, preferred_element_type=F32)
        for part in range(2):
            rows = slice(part * DH, (part + 1) * DH)
            scores = raw[rows] * SCALE
            sig = 0.5 * jnp.tanh(scores * 0.5) + 0.5
            keep = live[pl.ds(2 * i + part, 1), pl.ds(at, ROWS)]
            if diagonal:
                s = lax.broadcasted_iota(jnp.int32, (DH, ROWS), 0) + part * DH
                t = lax.broadcasted_iota(jnp.int32, (DH, ROWS), 1)
                keep = jnp.where(s <= t, keep, 0.0)
            fac = sig * keep
            weight = scores * fac
            wt[i, pl.ds(part * DH, DH), pl.ds(at, ROWS)] = weight.astype(BF16)
            dt[i, pl.ds(part * DH, DH), pl.ds(at, ROWS)] = fac + weight * (1.0 - sig)

    def scores_strip(i, carry):
        scores_tile(i, i, True)

        def body(j, c):
            scores_tile(i, j, False)
            return c

        lax.fori_loop(i + 1, SEQ, body, 0)
        return carry

    def value_strip(i, carry):
        def body(j, acc):
            at = pl.multiple_of(j * ROWS, ROWS)
            return acc + jnp.dot(
                wt[i, :, pl.ds(at, ROWS)], hist[G, j], preferred_element_type=F32
            )

        acc = lax.fori_loop(i, SEQ, body, jnp.zeros((ROWS, DH), F32))
        grads[DV, i] = acc.astype(BF16)
        return carry

    def score_grad_strip(i, carry):
        def body(j, acc):
            at = pl.multiple_of(j * ROWS, ROWS)
            products = lax.dot_general(
                hist[V, i], hist[G, j], nt, preferred_element_type=F32
            )
            score_grad = (products * dt[i, :, pl.ds(at, ROWS)]).astype(BF16)
            qacc[j] += lax.dot_general(
                score_grad, hist[K, i], tn, preferred_element_type=F32
            )
            return acc + jnp.dot(score_grad, hist[Q, j], preferred_element_type=F32)

        acc = lax.fori_loop(i, SEQ, body, jnp.zeros((ROWS, DH), F32))
        grads[DK, i] = (acc * SCALE).astype(BF16)
        return carry

    def send_grads(out):
        def body(k, carry):
            peer = lax.rem(sq + 4 + k, SEQ)
            src = grads.at[out, peer]
            dst = gath.at[
                2 * out + core,
                zed // 2,
                :,
                pl.ds(pl.multiple_of(lax.rem(zed, 2) * DH, DH), DH),
            ]
            recv_sem = grecv_sem.at[2 * out + core]

            @pl.when(k != 4)
            def _():
                remote(src, dst, gsend_sem.at[out], recv_sem, (dp, peer)).start()

            @pl.when(k == 4)
            def _():
                pltpu.make_async_copy(src, dst, recv_sem).start()

            return carry

        lax.fori_loop(0, SEQ, body, 0)

    def return_rows(out):
        for half in range(2):
            chunk = 2 * out + half
            landed(gath.at[chunk], grecv_sem.at[chunk])
            block = gath[chunk].reshape(2 * ROWS, QUART)
            osend[chunk] = (
                jnp.dot(spread[...], block, preferred_element_type=F32)
                .astype(BF16)
                .reshape(DP, PACK, QUART)
            )
            scatter_dp(osend, orecv, osend_sem, orecv_sem, chunk)

    stores = []

    def finish(out, target):
        for half in range(2):
            chunk = 2 * out + half
            landed(orecv.at[chunk], orecv_sem.at[chunk])

            def body(pair, carry):
                at = pl.multiple_of(pair * PACK, PACK)
                one = orecv[chunk, 2 * pair].astype(F32)
                two = orecv[chunk, 2 * pair + 1].astype(F32)
                lo = jnp.concatenate([one[:SLOT], two[:SLOT]], axis=0)
                hi = jnp.concatenate([one[SLOT:], two[SLOT:]], axis=0)
                base = half * HALF
                ostage[out, pl.ds(at, PACK), base : base + QUART] = lo.astype(BF16)
                ostage[out, pl.ds(at, PACK), base + QUART : base + HALF] = hi.astype(BF16)
                return carry

            lax.fori_loop(0, DP // 2, body, 0)
            store = pltpu.make_async_copy(
                ostage.at[out, :, pl.ds(half * HALF, HALF)],
                target.at[0, 0, :, pl.ds(half * HALF, HALF)],
                store_sem.at[1 + chunk],
            )
            store.start()
            stores.append(store)

    qacc[...] = jnp.zeros_like(qacc)
    gather_rows(Q)
    gather_rows(K)
    history(Q)
    history(K)
    lax.fori_loop(0, 3, scores_strip, 0)
    gather_rows(G)
    lax.fori_loop(3, SEQ, scores_strip, 0)
    history(G)
    lax.fori_loop(0, SEQ, value_strip, 0)
    send_grads(DV)
    gather_rows(V)
    history(V)
    return_rows(DV)
    lax.fori_loop(0, SEQ, score_grad_strip, 0)
    send_grads(DK)
    grads[DQ] = (qacc[...] * SCALE).astype(BF16)
    send_grads(DQ)
    return_rows(DK)
    return_rows(DQ)
    finish(DV, value_grad)
    finish(DK, key_grad)
    finish(DQ, query_grad)

    for chunk in range(8):
        left(dsend.at[chunk, pl.ds(0, DP - 1)], dsend_sem.at[chunk])
    for array in range(4):
        left(hist.at[array, pl.ds(0, SEQ - 1)], ssend_sem.at[array])
    for out in range(3):
        left(grads.at[out, pl.ds(0, SEQ - 1)], gsend_sem.at[out])
    for chunk in range(6):
        left(osend.at[chunk, pl.ds(0, DP - 1)], osend_sem.at[chunk])
    gate_store.wait()
    for store in stores:
        store.wait()


def local(queries, keys, values, gates, attended, out_grad, plan, hist_len, block_mask):
    hbm = pl.BlockSpec(memory_space=pl.ANY)
    smem = pl.BlockSpec(memory_space=pltpu.SMEM)
    vmem = pl.BlockSpec(memory_space=pltpu.VMEM)
    out = jax.ShapeDtypeStruct((1, 1, CAP, WIDTH), BF16)
    dma = pltpu.SemaphoreType.DMA
    return pl.pallas_call(
        kernel,
        out_shape=(out,) * 4,
        in_specs=[hbm] * 6 + [smem, smem, vmem],
        out_specs=(hbm,) * 4,
        scratch_shapes=[
            pltpu.VMEM((6, CAP, WIDTH), BF16),
            pltpu.VMEM((8, DP, PACK, QUART), BF16),
            pltpu.VMEM((8, DP, PACK, QUART), BF16),
            pltpu.VMEM((8, 2 * ROWS, QUART), BF16),
            pltpu.VMEM((4, SEQ, ROWS, DH), BF16),
            pltpu.VMEM((NBLK, LEN), F32),
            pltpu.VMEM((SEQ, ROWS, LEN), BF16),
            pltpu.VMEM((SEQ, ROWS, LEN), F32),
            pltpu.VMEM((SEQ, ROWS, DH), F32),
            pltpu.VMEM((3, SEQ, ROWS, DH), BF16),
            pltpu.VMEM((6, 2, ROWS, QUART), BF16),
            pltpu.VMEM((6, DP, PACK, QUART), BF16),
            pltpu.VMEM((6, DP, PACK, QUART), BF16),
            pltpu.VMEM((3, CAP, WIDTH), BF16),
            pltpu.VMEM((CAP, WIDTH), BF16),
            pltpu.VMEM((2 * ROWS, DP * PACK), BF16),
            pltpu.VMEM((DP * PACK, 2 * ROWS), BF16),
            dma((6,)),
            dma((7,)),
            dma((8,)),
            dma((8,)),
            dma((4,)),
            dma((4,)),
            dma((3,)),
            dma((6,)),
            dma((6,)),
            dma((6,)),
        ],
        compiler_params=pltpu.CompilerParams(
            collective_id=1, has_side_effects=True, vmem_limit_bytes=60 * 2**20
        ),
    )(queries, keys, values, gates, attended, out_grad, plan, hist_len, block_mask)


def solution(mesh):
    rows = P("dp", "seq", None, None)
    return jax.shard_map(
        local,
        mesh=mesh,
        in_specs=(rows,) * 6 + (P(None, "seq", None), P("dp"), P("dp", None, None)),
        out_specs=(rows,) * 4,
        check_vma=False,
    )
```

time: 375 us -> 121 us (0.32); the launches traced: 369 us -> 120 us
  Pallas kernels: 0 us -> 112 us
  waiting for transfers between devices: 92.7 us -> 0 us
  blocking collectives: 90.8 us -> 0 us
  matrix products: 82.7 us -> 0 us
  local copies, waits for them, and re-layouts: 66.8 us -> 5.85 us
  between operations: 15 us -> 1.3 us
  other arithmetic: 13.3 us -> 0 us
  starting transfers between devices: 7.89 us -> 0 us
    pallas_call x0 -> x1, Pallas kernels: none -> 112 us  [local(): pl.pallas_call(kernel, out_shape=(out,) * 4, in_specs=[hbm] * 6 + [smem,...]
    all_to_all x5 -> x0, blocking collectives: 90.8 us -> none  [the longest x1 21.1 us: local(): lax.all_to_all(pack(grads[0]), 'dp', split_axis=0, concat_axis=0, tiled=T...]
    dot_general x17 -> x0, matrix products: 82.7 us -> none  [the longest x2 21.6 us: pair_terms(): jnp.einsum('hts,shd->thd', score_grad, key_rows, preferred_element_type=j...]
    all_gather x4 -> x0, waiting for transfers between devices: 73 us -> none  [the longest x1 27.6 us: local(): shard_query = lax.all_gather(history[0], 'seq', axis=0, tiled=True)]
    slice x12 -> x0, local copies, waits for them, and re-layouts: 46 us -> none  [cut_rows(): return array[offset:offset + extent].reshape(extent, head_count, -1)]
    all_to_all x2 -> x0, waiting for transfers between devices: 18.3 us -> none  [the longest x1 12.4 us: local(): lax.all_to_all(pack(grads[2]), 'dp', split_axis=0, concat_axis=0, tiled=T...]
    gather x7 -> x0, local copies, waits for them, and re-layouts: 12.5 us -> none  [the longest x4 6.25 us: local(): jnp.take(array.reshape(group_count * slot_count, model_width), flat_index...]
    all_to_all x2 -> x0, starting transfers between devices: 7.26 us -> none  [the longest x1 3.63 us: local(): lax.all_to_all(flatten(queries).reshape(shape_slots), 'dp', split_axis=0,...]
  transfers between devices with their start and end apart: 6 -> 0, of which waited for: 5 -> 0; matrix products, arithmetic and copies ran while one was open for 17% -> 0% of each run, Pallas kernels for 0% -> 0%
where the time goes in v1:
time: 121 us; the launch traced here: 120 us
  Pallas kernels  112 us (93%)
  local copies, waits for them, and re-layouts  5.85 us (5%)
  between operations  1.3 us (1%)
    pallas_call x1, Pallas kernels, local(): pl.pallas_call(kernel, out_shape=(out,) * 4, in_specs=[hbm] * 6 + [smem,...  112 us
    unnamed x10, local copies, waits for them, and re-layouts  5.85 us

profile of v1, /device:TPU:0, one launch (start us, length us, event | category | flops | bytes accessed | tf_op | source)
XLA Modules:
  0.0 119.5 jit_solution(8263477092383026344)
XLA Ops:
  1.3 112.4 %shard_map.120 = (bf16[1,1,384,1024]{3,2,1,0:T(8,128)(2,1)}, bf16[1,1,384,1024]{3,2,1,0:T(8,128)(2,1)}, bf16[1,1,384,1024]{3,2,1,0:T(8,128)(2,1)}, bf16[1,1,384,1024]{3,2,1,0:T(8,128)(2,1)}) custom-call(bf16[1,1,384,1024]{3,2,1,0:T(8,128)(2,1)} %queries.1, bf16[1,1,384,1024]{3,2,1,0:T(8,128)(2,1)} %keys.1, bf16[1,1,384,1024]{3,2,1,0:T(8,128)(2,1)} %values.1, ...), custom_call_target="tpu_custom_call" | custom-call | tf_op jit(solution)/shard_map/pallas_call | solution.py:440
  113.7 0.0 copy-start.2
  113.7 2.1 %copy.18 = bf16[1,1,384,1024]{3,2,1,0:T(8,128)(2,1)} copy(bf16[1,1,384,1024]{3,2,1,0:T(8,128)(2,1)} %get-tuple-element.8) | data formatting | bytes 1572864
  115.8 0.0 copy-done.2
  115.8 0.0 copy-start.1
  115.8 0.9 copy.19
  116.7 0.5 copy-done.1
  117.2 0.0 copy-start
  117.2 0.9 copy.20
  118.1 0.5 copy-done
  118.7 0.9 copy.21
Async XLA Ops:
  113.7 2.1 %copy-start.2 = (bf16[1,1,384,1024]{3,2,1,0:T(8,128)(2,1)S(1)}, bf16[1,1,384,1024]{3,2,1,0:T(8,128)(2,1)}, u32[]{:S(2)}) copy-start(bf16[1,1,384,1024]{3,2,1,0:T(8,128)(2,1)} %get-tuple-element.9) | copy-start | bytes 2359300
  115.8 1.4 %copy-start.1 = (bf16[1,1,384,1024]{3,2,1,0:T(8,128)(2,1)S(1)}, bf16[1,1,384,1024]{3,2,1,0:T(8,128)(2,1)}, u32[]{:S(2)}) copy-start(bf16[1,1,384,1024]{3,2,1,0:T(8,128)(2,1)} %get-tuple-element.10) | copy-start | bytes 2359300
  117.2 1.4 %copy-start = (bf16[1,1,384,1024]{3,2,1,0:T(8,128)(2,1)S(1)}, bf16[1,1,384,1024]{3,2,1,0:T(8,128)(2,1)}, u32[]{:S(2)}) copy-start(bf16[1,1,384,1024]{3,2,1,0:T(8,128)(2,1)} %get-tuple-element.11) | copy-start | bytes 2359300

commit v2 on v1

--- a/solution.py
+++ b/solution.py
@@ -22,6 +22,8 @@
 HALF = 512
 QUART = 256
 SCALE = DH ** (-0.5)
+TILE = 512
+TILES = LEN // TILE
 
 Q, K, G, V = 0, 1, 2, 3
 DV, DK, DQ = 0, 1, 2
@@ -49,7 +51,7 @@
     live,
     wt,
     dt,
-    qacc,
+    key_t,
     grads,
     gath,
     osend,
@@ -246,53 +248,59 @@
         ((kept > 0.5) | (onehot > 0.5)) & (pos < length), inverse, 0.0
     )
 
-    def gather_rows(array):
-        for half in range(2):
-            chunk = 2 * array + half
-            landed(drecv.at[chunk], drecv_sem.at[chunk])
-            block = drecv[chunk].reshape(DP * PACK, QUART)
-            comp[chunk] = jnp.dot(
-                place[...], block, preferred_element_type=F32
-            ).astype(BF16)
-            for to in range(4):
-                src = comp.at[
-                    chunk, pl.ds(to // 2 * ROWS, ROWS), pl.ds(to % 2 * DH, DH)
-                ]
-                dst = hist.at[array, sq]
-                peer = 2 * to + half
-
-                @pl.when(sq != peer)
-                def _():
-                    remote(
-                        src, dst, ssend_sem.at[array], srecv_sem.at[array], (dp, peer)
-                    ).start()
-
-                @pl.when(sq == peer)
-                def _():
-                    pltpu.make_async_copy(src, dst, srecv_sem.at[array]).start()
+    def gather_rows(array, half):
+        chunk = 2 * array + half
+        landed(drecv.at[chunk], drecv_sem.at[chunk])
+        block = drecv[chunk].reshape(DP * PACK, QUART)
+        comp[chunk] = jnp.dot(place[...], block, preferred_element_type=F32).astype(
+            BF16
+        )
+        for to in range(4):
+            src = comp.at[
+                chunk, pl.ds(to // 2 * ROWS, ROWS), pl.ds(to % 2 * DH, DH)
+            ]
+            dst = hist.at[array, sq]
+            peer = 2 * to + half
+
+            @pl.when(sq != peer)
+            def _():
+                remote(
+                    src, dst, ssend_sem.at[array], srecv_sem.at[array], (dp, peer)
+                ).start()
+
+            @pl.when(sq == peer)
+            def _():
+                pltpu.make_async_copy(src, dst, srecv_sem.at[array]).start()
 
     def history(array):
         landed(hist.at[array], srecv_sem.at[array])
 
     nt = (((1,), (1,)), ((), ()))
-    tn = (((0,), (0,)), ((), ()))
+
+    def tile_rows(array, i):
+        return hist[array, pl.ds(2 * i, 2)].reshape(TILE, DH)
 
     def scores_tile(i, j, diagonal):
-        at = pl.multiple_of(j * ROWS, ROWS)
-        raw = lax.dot_general(hist[K, i], hist[Q, j], nt, preferred_element_type=F32)
-        for part in range(2):
-            rows = slice(part * DH, (part + 1) * DH)
-            scores = raw[rows] * SCALE
-            sig = 0.5 * jnp.tanh(scores * 0.5) + 0.5
-            keep = live[pl.ds(2 * i + part, 1), pl.ds(at, ROWS)]
+        cols = pl.ds(pl.multiple_of(j * TILE, TILE), TILE)
+        query = tile_rows(Q, j)
+        key = tile_rows(K, i)
+        for part in range(TILE // DH):
+            base = part * DH
+            raw = lax.dot_general(
+                key[base : base + DH], query, nt, preferred_element_type=F32
+            )
+            scores = raw * SCALE
+            sig = 0.5 * jnp.tanh(raw * (0.5 * SCALE)) + 0.5
+            keep = live[pl.ds(TILE // DH * i + part, 1), cols]
             if diagonal:
-                s = lax.broadcasted_iota(jnp.int32, (DH, ROWS), 0) + part * DH
-                t = lax.broadcasted_iota(jnp.int32, (DH, ROWS), 1)
+                s = lax.broadcasted_iota(jnp.int32, (DH, TILE), 0) + base
+                t = lax.broadcasted_iota(jnp.int32, (DH, TILE), 1)
                 keep = jnp.where(s <= t, keep, 0.0)
             fac = sig * keep
             weight = scores * fac
-            wt[i, pl.ds(part * DH, DH), pl.ds(at, ROWS)] = weight.astype(BF16)
-            dt[i, pl.ds(part * DH, DH), pl.ds(at, ROWS)] = fac + weight * (1.0 - sig)
+            rows = pl.ds(pl.multiple_of(i * TILE + base, DH), DH)
+            wt[rows, cols] = weight.astype(BF16)
+            dt[rows, cols] = fac + weight * (1.0 - sig)
 
     def scores_strip(i, carry):
         scores_tile(i, i, True)
@@ -301,35 +309,45 @@
             scores_tile(i, j, False)
             return c
 
-        lax.fori_loop(i + 1, SEQ, body, 0)
+        lax.fori_loop(i + 1, TILES, body, 0)
         return carry
 
-    def value_strip(i, carry):
-        def body(j, acc):
-            at = pl.multiple_of(j * ROWS, ROWS)
-            return acc + jnp.dot(
-                wt[i, :, pl.ds(at, ROWS)], hist[G, j], preferred_element_type=F32
-            )
-
-        acc = lax.fori_loop(i, SEQ, body, jnp.zeros((ROWS, DH), F32))
-        grads[DV, i] = acc.astype(BF16)
+    def later_sum(out, array, scale):
+        for i in range(TILES):
+            acc = jnp.dot(
+                wt[i * TILE : (i + 1) * TILE, i * TILE :],
+                hist[array, 2 * i :].reshape(LEN - i * TILE, DH),
+                preferred_element_type=F32,
+            )
+            grads[out, 2 * i : 2 * i + 2] = (
+                (acc * scale).astype(BF16).reshape(2, ROWS, DH)
+            )
+
+    def score_grad_strip(i, carry):
+        rows = pl.ds(pl.multiple_of(i * TILE, TILE), TILE)
+        value = tile_rows(V, i)
+
+        def body(j, c):
+            cols = pl.ds(pl.multiple_of(j * TILE, TILE), TILE)
+            products = lax.dot_general(
+                value, tile_rows(G, j), nt, preferred_element_type=F32
+            )
+            wt[rows, cols] = (products * dt[rows, cols]).astype(BF16)
+            return c
+
+        lax.fori_loop(i, TILES, body, 0)
         return carry
 
-    def score_grad_strip(i, carry):
-        def body(j, acc):
-            at = pl.multiple_of(j * ROWS, ROWS)
-            products = lax.dot_general(
-                hist[V, i], hist[G, j], nt, preferred_element_type=F32
-            )
-            score_grad = (products * dt[i, :, pl.ds(at, ROWS)]).astype(BF16)
-            qacc[j] += lax.dot_general(
-                score_grad, hist[K, i], tn, preferred_element_type=F32
-            )
-            return acc + jnp.dot(score_grad, hist[Q, j], preferred_element_type=F32)
-
-        acc = lax.fori_loop(i, SEQ, body, jnp.zeros((ROWS, DH), F32))
-        grads[DK, i] = (acc * SCALE).astype(BF16)
-        return carry
+    def query_sum():
+        for j in range(TILES):
+            acc = jnp.dot(
+                key_t[:, : (j + 1) * TILE],
+                wt[: (j + 1) * TILE, j * TILE : (j + 1) * TILE],
+                preferred_element_type=F32,
+            )
+            grads[DQ, 2 * j : 2 * j + 2] = (
+                (acc * SCALE).T.astype(BF16).reshape(2, ROWS, DH)
+            )
 
     def send_grads(out):
         def body(k, carry):
@@ -394,23 +412,28 @@
             store.start()
             stores.append(store)
 
-    qacc[...] = jnp.zeros_like(qacc)
-    gather_rows(Q)
-    gather_rows(K)
+    gather_rows(Q, 0)
+    gather_rows(Q, 1)
+    gather_rows(K, 0)
+    gather_rows(K, 1)
+    gather_rows(G, 0)
     history(Q)
     history(K)
-    lax.fori_loop(0, 3, scores_strip, 0)
-    gather_rows(G)
-    lax.fori_loop(3, SEQ, scores_strip, 0)
+    lax.fori_loop(0, 1, scores_strip, 0)
+    gather_rows(G, 1)
+    lax.fori_loop(1, TILES, scores_strip, 0)
     history(G)
-    lax.fori_loop(0, SEQ, value_strip, 0)
+    later_sum(DV, G, 1.0)
     send_grads(DV)
-    gather_rows(V)
+    gather_rows(V, 0)
+    gather_rows(V, 1)
+    key_t[...] = hist[K].reshape(LEN, DH).astype(F32).T.astype(BF16)
+    return_rows(DV)
     history(V)
-    return_rows(DV)
-    lax.fori_loop(0, SEQ, score_grad_strip, 0)
+    lax.fori_loop(0, TILES, score_grad_strip, 0)
+    later_sum(DK, Q, SCALE)
     send_grads(DK)
-    grads[DQ] = (qacc[...] * SCALE).astype(BF16)
+    query_sum()
     send_grads(DQ)
     return_rows(DK)
     return_rows(DQ)
@@ -449,9 +472,9 @@
             pltpu.VMEM((8, 2 * ROWS, QUART), BF16),
             pltpu.VMEM((4, SEQ, ROWS, DH), BF16),
             pltpu.VMEM((NBLK, LEN), F32),
-            pltpu.VMEM((SEQ, ROWS, LEN), BF16),
-            pltpu.VMEM((SEQ, ROWS, LEN), F32),
-            pltpu.VMEM((SEQ, ROWS, DH), F32),
+            pltpu.VMEM((LEN, LEN), BF16),
+            pltpu.VMEM((LEN, LEN), F32),
+            pltpu.VMEM((DH, LEN), BF16),
             pltpu.VMEM((3, SEQ, ROWS, DH), BF16),
             pltpu.VMEM((6, 2, ROWS, QUART), BF16),
             pltpu.VMEM((6, DP, PACK, QUART), BF16),

time: 121 us -> 97.9 us (0.81)
  Pallas kernels: 112 us -> 89.4 us
    pallas_call x1, Pallas kernels: 112 us -> 89.4 us  [local(): pl.pallas_call(kernel, out_shape=(out,) * 4, in_specs=[hbm] * 6 + [smem,...]
where the time goes in v2:
time: 97.9 us; the launch traced here: 96.5 us
  Pallas kernels  89.4 us (91%)
  local copies, waits for them, and re-layouts  5.85 us (6%)
  between operations  1.3 us (1%)
    pallas_call x1, Pallas kernels, local(): pl.pallas_call(kernel, out_shape=(out,) * 4, in_specs=[hbm] * 6 + [smem,...  89.4 us
    unnamed x10, local copies, waits for them, and re-layouts  5.85 us

profile of v2, /device:TPU:0, one launch (start us, length us, event | category | flops | bytes accessed | tf_op | source)
XLA Modules:
  0.0 96.5 jit_solution(8268572604935448062)
XLA Ops:
  1.3 89.4 %shard_map.120 = (bf16[1,1,384,1024]{3,2,1,0:T(8,128)(2,1)}, bf16[1,1,384,1024]{3,2,1,0:T(8,128)(2,1)}, bf16[1,1,384,1024]{3,2,1,0:T(8,128)(2,1)}, bf16[1,1,384,1024]{3,2,1,0:T(8,128)(2,1)}) custom-call(bf16[1,1,384,1024]{3,2,1,0:T(8,128)(2,1)} %queries.1, bf16[1,1,384,1024]{3,2,1,0:T(8,128)(2,1)} %keys.1, bf16[1,1,384,1024]{3,2,1,0:T(8,128)(2,1)} %values.1, ...), custom_call_target="tpu_custom_call" | custom-call | tf_op jit(solution)/shard_map/pallas_call | solution.py:463
  90.7 0.0 copy-start.2
  90.7 2.1 %copy.18 = bf16[1,1,384,1024]{3,2,1,0:T(8,128)(2,1)} copy(bf16[1,1,384,1024]{3,2,1,0:T(8,128)(2,1)} %get-tuple-element.8) | data formatting | bytes 1572864
  92.8 0.0 copy-done.2
  92.8 0.0 copy-start.1
  92.8 0.9 copy.19
  93.7 0.5 copy-done.1
  94.2 0.0 copy-start
  94.2 0.9 copy.20
  95.1 0.5 copy-done
  95.7 0.9 copy.21
Async XLA Ops:
  90.7 2.1 %copy-start.2 = (bf16[1,1,384,1024]{3,2,1,0:T(8,128)(2,1)S(1)}, bf16[1,1,384,1024]{3,2,1,0:T(8,128)(2,1)}, u32[]{:S(2)}) copy-start(bf16[1,1,384,1024]{3,2,1,0:T(8,128)(2,1)} %get-tuple-element.9) | copy-start | bytes 2359300
  92.8 1.4 %copy-start.1 = (bf16[1,1,384,1024]{3,2,1,0:T(8,128)(2,1)S(1)}, bf16[1,1,384,1024]{3,2,1,0:T(8,128)(2,1)}, u32[]{:S(2)}) copy-start(bf16[1,1,384,1024]{3,2,1,0:T(8,128)(2,1)} %get-tuple-element.10) | copy-start | bytes 2359300
  94.2 1.4 %copy-start = (bf16[1,1,384,1024]{3,2,1,0:T(8,128)(2,1)S(1)}, bf16[1,1,384,1024]{3,2,1,0:T(8,128)(2,1)}, u32[]{:S(2)}) copy-start(bf16[1,1,384,1024]{3,2,1,0:T(8,128)(2,1)} %get-tuple-element.11) | copy-start | bytes 2359300

commit v3 on v2

--- a/solution.py
+++ b/solution.py
@@ -39,9 +39,7 @@
     plan,
     hist_len,
     block_mask,
-    query_grad,
-    key_grad,
-    value_grad,
+    orecv,
     gate_grad,
     stage,
     dsend,
@@ -55,8 +53,6 @@
     grads,
     gath,
     osend,
-    orecv,
-    ostage,
     gstage,
     place,
     spread,
@@ -90,9 +86,6 @@
         )
         return carry
 
-    lax.fori_loop(1, DP, greet_dp, 0)
-    lax.fori_loop(1, SEQ, greet_seq, 0)
-
     sources = (queries, keys, attended, gates, out_grad, values)
     loads = [
         pltpu.make_async_copy(src.at[0, 0], stage.at[i], load_sem.at[i])
@@ -100,6 +93,9 @@
     ]
     for load in loads:
         load.start()
+
+    lax.fori_loop(1, DP, greet_dp, 0)
+    lax.fori_loop(1, SEQ, greet_seq, 0)
 
     def remote(src, dst, send_sem, recv_sem, target):
         return pltpu.make_async_remote_copy(
@@ -162,15 +158,14 @@
 
         lax.fori_loop(0, DP // 2, body, 0)
 
-    def send(array):
-        for half in range(2):
-            scatter_dp(dsend, drecv, dsend_sem, drecv_sem, 2 * array + half)
+    def send(array, half):
+        scatter_dp(dsend, drecv, dsend_sem, drecv_sem, 2 * array + half)
 
     pack(Q, 0)
     pl.semaphore_wait(barrier, DP - 1 + SEQ - 1)
-    send(Q)
+    send(Q, 0)
     pack(K, 1)
-    send(K)
+    send(K, 0)
 
     for i in (2, 3, 4):
         loads[i].wait()
@@ -197,11 +192,11 @@
         return carry
 
     lax.fori_loop(0, DP // 2, norm_body, 0)
-    send(G)
-    gate_store = pltpu.make_async_copy(gstage, gate_grad.at[0, 0], store_sem.at[0])
+    send(G, 0)
+    gate_store = pltpu.make_async_copy(gstage, gate_grad, store_sem.at[0])
     gate_store.start()
     pack(V, 5)
-    send(V)
+    send(V, 0)
 
     lane768 = lax.broadcasted_iota(jnp.int32, (1, DP * PACK), 1)
     lane512 = lax.broadcasted_iota(jnp.int32, (1, 2 * ROWS), 1)
@@ -339,6 +334,7 @@
         return carry
 
     def query_sum():
+        key_t[...] = hist[K].reshape(LEN, DH).astype(F32).T.astype(BF16)
         for j in range(TILES):
             acc = jnp.dot(
                 key_t[:, : (j + 1) * TILE],
@@ -373,73 +369,89 @@
 
         lax.fori_loop(0, SEQ, body, 0)
 
-    def return_rows(out):
-        for half in range(2):
-            chunk = 2 * out + half
-            landed(gath.at[chunk], grecv_sem.at[chunk])
-            block = gath[chunk].reshape(2 * ROWS, QUART)
-            osend[chunk] = (
-                jnp.dot(spread[...], block, preferred_element_type=F32)
-                .astype(BF16)
-                .reshape(DP, PACK, QUART)
-            )
-            scatter_dp(osend, orecv, osend_sem, orecv_sem, chunk)
-
-    stores = []
-
-    def finish(out, target):
-        for half in range(2):
-            chunk = 2 * out + half
-            landed(orecv.at[chunk], orecv_sem.at[chunk])
-
-            def body(pair, carry):
-                at = pl.multiple_of(pair * PACK, PACK)
-                one = orecv[chunk, 2 * pair].astype(F32)
-                two = orecv[chunk, 2 * pair + 1].astype(F32)
-                lo = jnp.concatenate([one[:SLOT], two[:SLOT]], axis=0)
-                hi = jnp.concatenate([one[SLOT:], two[SLOT:]], axis=0)
-                base = half * HALF
-                ostage[out, pl.ds(at, PACK), base : base + QUART] = lo.astype(BF16)
-                ostage[out, pl.ds(at, PACK), base + QUART : base + HALF] = hi.astype(BF16)
-                return carry
-
-            lax.fori_loop(0, DP // 2, body, 0)
-            store = pltpu.make_async_copy(
-                ostage.at[out, :, pl.ds(half * HALF, HALF)],
-                target.at[0, 0, :, pl.ds(half * HALF, HALF)],
-                store_sem.at[1 + chunk],
-            )
-            store.start()
-            stores.append(store)
+    def return_rows(out, half):
+        chunk = 2 * out + half
+        landed(gath.at[chunk], grecv_sem.at[chunk])
+        block = gath[chunk].reshape(2 * ROWS, QUART)
+        osend[chunk] = (
+            jnp.dot(spread[...], block, preferred_element_type=F32)
+            .astype(BF16)
+            .reshape(DP, PACK, QUART)
+        )
+        scatter_dp(osend, orecv, osend_sem, orecv_sem, chunk)
 
     gather_rows(Q, 0)
+    send(Q, 1)
+    gather_rows(K, 0)
+    send(K, 1)
+    gather_rows(G, 0)
+    send(G, 1)
+
+    @pl.when(core == 0)
+    def _():
+        history(Q)
+        history(K)
+        lax.fori_loop(0, 1, scores_strip, 0)
+
+    gather_rows(V, 0)
+    send(V, 1)
+
+    @pl.when(core == 0)
+    def _():
+        lax.fori_loop(1, TILES, scores_strip, 0)
+        history(G)
+        later_sum(DV, G, 1.0)
+        send_grads(DV)
+
     gather_rows(Q, 1)
-    gather_rows(K, 0)
+
+    @pl.when(core == 0)
+    def _():
+        history(V)
+        lax.fori_loop(0, TILES, score_grad_strip, 0)
+        later_sum(DK, Q, SCALE)
+        send_grads(DK)
+
     gather_rows(K, 1)
-    gather_rows(G, 0)
-    history(Q)
-    history(K)
-    lax.fori_loop(0, 1, scores_strip, 0)
+
+    @pl.when(core == 0)
+    def _():
+        query_sum()
+        send_grads(DQ)
+
     gather_rows(G, 1)
-    lax.fori_loop(1, TILES, scores_strip, 0)
-    history(G)
-    later_sum(DV, G, 1.0)
-    send_grads(DV)
-    gather_rows(V, 0)
+
+    @pl.when(core == 1)
+    def _():
+        history(Q)
+        history(K)
+        lax.fori_loop(0, 1, scores_strip, 0)
+
     gather_rows(V, 1)
-    key_t[...] = hist[K].reshape(LEN, DH).astype(F32).T.astype(BF16)
-    return_rows(DV)
-    history(V)
-    lax.fori_loop(0, TILES, score_grad_strip, 0)
-    later_sum(DK, Q, SCALE)
-    send_grads(DK)
-    query_sum()
-    send_grads(DQ)
-    return_rows(DK)
-    return_rows(DQ)
-    finish(DV, value_grad)
-    finish(DK, key_grad)
-    finish(DQ, query_grad)
+    return_rows(DV, 0)
+    return_rows(DK, 0)
+
+    @pl.when(core == 1)
+    def _():
+        lax.fori_loop(1, TILES, scores_strip, 0)
+        history(G)
+        later_sum(DV, G, 1.0)
+        send_grads(DV)
+
+    return_rows(DQ, 0)
+
+    @pl.when(core == 1)
+    def _():
+        history(V)
+        lax.fori_loop(0, TILES, score_grad_strip, 0)
+        later_sum(DK, Q, SCALE)
+        send_grads(DK)
+        query_sum()
+        send_grads(DQ)
+
+    return_rows(DV, 1)
+    return_rows(DK, 1)
+    return_rows(DQ, 1)
 
     for chunk in range(8):
         left(dsend.at[chunk, pl.ds(0, DP - 1)], dsend_sem.at[chunk])
@@ -448,8 +460,48 @@
     for out in range(3):
         left(grads.at[out, pl.ds(0, SEQ - 1)], gsend_sem.at[out])
     for chunk in range(6):
+        landed(orecv.at[chunk], orecv_sem.at[chunk])
         left(osend.at[chunk, pl.ds(0, DP - 1)], osend_sem.at[chunk])
     gate_store.wait()
+
+
+def unpack(
+    moved, gate_in, query_grad, key_grad, value_grad, gate_grad, block, ready, gate, load_sem, store_sem
+):
+    loads = [
+        pltpu.make_async_copy(moved.at[chunk], block.at[chunk], load_sem.at[chunk])
+        for chunk in range(6)
+    ]
+    loads.append(pltpu.make_async_copy(gate_in, gate, load_sem.at[6]))
+    for load in loads:
+        load.start()
+    stores = []
+    for chunk in range(6):
+        loads[chunk].wait()
+
+        def body(pair, carry):
+            at = pl.multiple_of(pair * PACK, PACK)
+            one = block[chunk, 2 * pair].astype(F32)
+            two = block[chunk, 2 * pair + 1].astype(F32)
+            lo = jnp.concatenate([one[:SLOT], two[:SLOT]], axis=0)
+            hi = jnp.concatenate([one[SLOT:], two[SLOT:]], axis=0)
+            ready[chunk, pl.ds(at, PACK), :QUART] = lo.astype(BF16)
+            ready[chunk, pl.ds(at, PACK), QUART:] = hi.astype(BF16)
+            return carry
+
+        lax.fori_loop(0, DP // 2, body, 0, unroll=True)
+        target = (value_grad, key_grad, query_grad)[chunk // 2]
+        store = pltpu.make_async_copy(
+            ready.at[chunk],
+            target.at[0, 0, :, pl.ds(chunk % 2 * HALF, HALF)],
+            store_sem.at[chunk],
+        )
+        store.start()
+        stores.append(store)
+    loads[6].wait()
+    store = pltpu.make_async_copy(gate, gate_grad.at[0, 0], store_sem.at[6])
+    store.start()
+    stores.append(store)
     for store in stores:
         store.wait()
 
@@ -459,12 +511,14 @@
     smem = pl.BlockSpec(memory_space=pltpu.SMEM)
     vmem = pl.BlockSpec(memory_space=pltpu.VMEM)
     out = jax.ShapeDtypeStruct((1, 1, CAP, WIDTH), BF16)
+    arrived = jax.ShapeDtypeStruct((6, DP, PACK, QUART), BF16)
+    gate_out = jax.ShapeDtypeStruct((CAP, WIDTH), BF16)
     dma = pltpu.SemaphoreType.DMA
-    return pl.pallas_call(
+    moved, gate_grad = pl.pallas_call(
         kernel,
-        out_shape=(out,) * 4,
+        out_shape=(arrived, gate_out),
         in_specs=[hbm] * 6 + [smem, smem, vmem],
-        out_specs=(hbm,) * 4,
+        out_specs=(hbm,) * 2,
         scratch_shapes=[
             pltpu.VMEM((6, CAP, WIDTH), BF16),
             pltpu.VMEM((8, DP, PACK, QUART), BF16),
@@ -478,13 +532,11 @@
             pltpu.VMEM((3, SEQ, ROWS, DH), BF16),
             pltpu.VMEM((6, 2, ROWS, QUART), BF16),
             pltpu.VMEM((6, DP, PACK, QUART), BF16),
-            pltpu.VMEM((6, DP, PACK, QUART), BF16),
-            pltpu.VMEM((3, CAP, WIDTH), BF16),
             pltpu.VMEM((CAP, WIDTH), BF16),
             pltpu.VMEM((2 * ROWS, DP * PACK), BF16),
             pltpu.VMEM((DP * PACK, 2 * ROWS), BF16),
             dma((6,)),
-            dma((7,)),
+            dma((1,)),
             dma((8,)),
             dma((8,)),
             dma((4,)),
@@ -498,6 +550,20 @@
             collective_id=1, has_side_effects=True, vmem_limit_bytes=60 * 2**20
         ),
     )(queries, keys, values, gates, attended, out_grad, plan, hist_len, block_mask)
+    return pl.pallas_call(
+        unpack,
+        out_shape=(out,) * 4,
+        in_specs=[hbm] * 2,
+        out_specs=(hbm,) * 4,
+        scratch_shapes=[
+            pltpu.VMEM((6, DP, PACK, QUART), BF16),
+            pltpu.VMEM((6, CAP, HALF), BF16),
+            pltpu.VMEM((CAP, WIDTH), BF16),
+            dma((7,)),
+            dma((7,)),
+        ],
+        compiler_params=pltpu.CompilerParams(vmem_limit_bytes=60 * 2**20),
+    )(moved, gate_grad)
 
 
 def solution(mesh):

time: 97.9 us -> 87.2 us (0.89)
  local copies, waits for them, and re-layouts: 5.85 us -> 0 us
  Pallas kernels: 89.4 us -> 85.4 us
    unnamed x10 -> x0, local copies, waits for them, and re-layouts: 5.85 us -> none
    pallas_call x1 -> x2, Pallas kernels: 89.4 us -> 85.4 us  [the longest x1 82.5 us: local(): pl.pallas_call(kernel, out_shape=(arrived, gate_out), in_specs=[hbm] * 6...]
where the time goes in v3:
time: 87.2 us; the launch traced here: 86.8 us
  Pallas kernels  85.4 us (98%)
  between operations  1.45 us (2%)
    pallas_call x1, Pallas kernels, local(): pl.pallas_call(kernel, out_shape=(arrived, gate_out), in_specs=[hbm] * 6...  82.5 us
    pallas_call x1, Pallas kernels, local(): pl.pallas_call(unpack, out_shape=(out,) * 4, in_specs=[hbm] * 2, out_spec...  2.85 us

profile of v3, /device:TPU:0, one launch (start us, length us, event | category | flops | bytes accessed | tf_op | source)
XLA Modules:
  0.0 86.8 jit_solution(3293363637851371574)
XLA Ops:
  1.3 82.5 %shard_map.120 = (bf16[6,16,48,256]{3,2,1,0:T(8,128)(2,1)}, bf16[384,1024]{1,0:T(8,128)(2,1)}) custom-call(bf16[1,1,384,1024]{3,2,1,0:T(8,128)(2,1)} %queries.1, bf16[1,1,384,1024]{3,2,1,0:T(8,128)(2,1)} %keys.1, bf16[1,1,384,1024]{3,2,1,0:T(8,128)(2,1)} %values.1, bf16[1,1,384,1024]{3,2,1,0:T(8,128)(2,1)} %gates.1, bf16[1,1,384,1024]{3,2,1,0:T(8,128)(2,1)} %attended.1, ...), custom_call_target="tpu_custom_call" | custom-call | tf_op jit(solution)/shard_map/pallas_call | solution.py:517
  83.8 2.9 %shard_map.121 = (bf16[1,1,384,1024]{3,2,1,0:T(8,128)(2,1)}, bf16[1,1,384,1024]{3,2,1,0:T(8,128)(2,1)}, bf16[1,1,384,1024]{3,2,1,0:T(8,128)(2,1)}, bf16[1,1,384,1024]{3,2,1,0:T(8,128)(2,1)}) custom-call(bf16[6,16,48,256]{3,2,1,0:T(8,128)(2,1)} %get-tuple-element.6.moved, bf16[384,1024]{1,0:T(8,128)(2,1)} %get-tuple-element.7.gate_in), custom_call_target="tpu_custom_call" | custom-call | tf_op jit(solution)/shard_map/pallas_call | solution.py:553

commit v4 on v3

--- a/solution.py
+++ b/solution.py
@@ -192,11 +192,9 @@
         return carry
 
     lax.fori_loop(0, DP // 2, norm_body, 0)
-    send(G, 0)
     gate_store = pltpu.make_async_copy(gstage, gate_grad, store_sem.at[0])
     gate_store.start()
     pack(V, 5)
-    send(V, 0)
 
     lane768 = lax.broadcasted_iota(jnp.int32, (1, DP * PACK), 1)
     lane512 = lax.broadcasted_iota(jnp.int32, (1, 2 * ROWS), 1)
@@ -250,9 +248,12 @@
         comp[chunk] = jnp.dot(place[...], block, preferred_element_type=F32).astype(
             BF16
         )
-        for to in range(4):
+        for k in range(4):
+            to = lax.rem(zed + 2 + k, 4)
             src = comp.at[
-                chunk, pl.ds(to // 2 * ROWS, ROWS), pl.ds(to % 2 * DH, DH)
+                chunk,
+                pl.ds(pl.multiple_of(to // 2 * ROWS, ROWS), ROWS),
+                pl.ds(pl.multiple_of(lax.rem(to, 2) * DH, DH), DH),
             ]
             dst = hist.at[array, sq]
             peer = 2 * to + half
@@ -381,11 +382,11 @@
         scatter_dp(osend, orecv, osend_sem, orecv_sem, chunk)
 
     gather_rows(Q, 0)
+    send(G, 0)
+    gather_rows(K, 0)
+    send(V, 0)
+    gather_rows(G, 0)
     send(Q, 1)
-    gather_rows(K, 0)
-    send(K, 1)
-    gather_rows(G, 0)
-    send(G, 1)
 
     @pl.when(core == 0)
     def _():
@@ -394,7 +395,7 @@
         lax.fori_loop(0, 1, scores_strip, 0)
 
     gather_rows(V, 0)
-    send(V, 1)
+    send(K, 1)
 
     @pl.when(core == 0)
     def _():
@@ -404,18 +405,20 @@
         send_grads(DV)
 
     gather_rows(Q, 1)
+    send(G, 1)
 
     @pl.when(core == 0)
     def _():
         history(V)
         lax.fori_loop(0, TILES, score_grad_strip, 0)
+
+    gather_rows(K, 1)
+    send(V, 1)
+
+    @pl.when(core == 0)
+    def _():
         later_sum(DK, Q, SCALE)
         send_grads(DK)
-
-    gather_rows(K, 1)
-
-    @pl.when(core == 0)
-    def _():
         query_sum()
         send_grads(DQ)
 

time: 87.2 us -> 84.9 us (0.974)
  Pallas kernels: 85.4 us -> 83 us
    pallas_call x1, Pallas kernels: 82.5 us -> 80.1 us  [local(): pl.pallas_call(kernel, out_shape=(arrived, gate_out), in_specs=[hbm] * 6...]
where the time goes in v4:
time: 84.9 us; the launch traced here: 84.4 us
  Pallas kernels  83 us (98%)
  between operations  1.45 us (2%)
    pallas_call x1, Pallas kernels, local(): pl.pallas_call(kernel, out_shape=(arrived, gate_out), in_specs=[hbm] * 6...  80.1 us
    pallas_call x1, Pallas kernels, local(): pl.pallas_call(unpack, out_shape=(out,) * 4, in_specs=[hbm] * 2, out_spec...  2.85 us

profile of v4, /device:TPU:0, one launch (start us, length us, event | category | flops | bytes accessed | tf_op | source)
XLA Modules:
  0.0 84.4 jit_solution(16396543704264644247)
XLA Ops:
  1.3 80.1 %shard_map.120 = (bf16[6,16,48,256]{3,2,1,0:T(8,128)(2,1)}, bf16[384,1024]{1,0:T(8,128)(2,1)}) custom-call(bf16[1,1,384,1024]{3,2,1,0:T(8,128)(2,1)} %queries.1, bf16[1,1,384,1024]{3,2,1,0:T(8,128)(2,1)} %keys.1, bf16[1,1,384,1024]{3,2,1,0:T(8,128)(2,1)} %values.1, bf16[1,1,384,1024]{3,2,1,0:T(8,128)(2,1)} %gates.1, bf16[1,1,384,1024]{3,2,1,0:T(8,128)(2,1)} %attended.1, ...), custom_call_target="tpu_custom_call" | custom-call | tf_op jit(solution)/shard_map/pallas_call | solution.py:520
  81.4 2.9 %shard_map.121 = (bf16[1,1,384,1024]{3,2,1,0:T(8,128)(2,1)}, bf16[1,1,384,1024]{3,2,1,0:T(8,128)(2,1)}, bf16[1,1,384,1024]{3,2,1,0:T(8,128)(2,1)}, bf16[1,1,384,1024]{3,2,1,0:T(8,128)(2,1)}) custom-call(bf16[6,16,48,256]{3,2,1,0:T(8,128)(2,1)} %get-tuple-element.6.moved, bf16[384,1024]{1,0:T(8,128)(2,1)} %get-tuple-element.7.gate_in), custom_call_target="tpu_custom_call" | custom-call | tf_op jit(solution)/shard_map/pallas_call | solution.py:556

commit v5 on v4

--- a/solution.py
+++ b/solution.py
@@ -24,6 +24,11 @@
 SCALE = DH ** (-0.5)
 TILE = 512
 TILES = LEN // TILE
+
+FAR_FIRST = sorted(
+    [(i // 4, i % 4) for i in range(1, DP)],
+    key=lambda step: -sum(min(i, 4 - i) for i in step),
+)
 
 Q, K, G, V = 0, 1, 2, 3
 DV, DK, DQ = 0, 1, 2
@@ -72,6 +77,9 @@
     row_x, row_y = dp // 4, lax.rem(dp, 4)
     zed, core = sq // 2, lax.rem(sq, 2)
 
+    column = [4 * lax.rem(row_x + i, 4) for i in range(4)]
+    line = [lax.rem(row_y + i, 4) for i in range(4)]
+
     barrier = pltpu.get_barrier_semaphore()
 
     def greet_dp(k, carry):
@@ -114,29 +122,18 @@
         remote(ref, ref, sem, sem, (dp, sq)).wait_send()
 
     def scatter_dp(src, dst, send_sems, recv_sems, chunk):
-        def body(k, carry):
-            off = k ^ 10
-            peer = lax.rem(row_x + off // 4, 4) * 4 + lax.rem(row_y + lax.rem(off, 4), 4)
-
-            @pl.when(k != 10)
-            def _():
-                remote(
-                    src.at[chunk, peer],
-                    dst.at[chunk, dp],
-                    send_sems.at[chunk],
-                    recv_sems.at[chunk],
-                    (peer, sq),
-                ).start()
-
-            @pl.when(k == 10)
-            def _():
-                pltpu.make_async_copy(
-                    src.at[chunk, dp], dst.at[chunk, dp], recv_sems.at[chunk]
-                ).start()
-
-            return carry
-
-        lax.fori_loop(0, DP, body, 0)
+        pltpu.make_async_copy(
+            src.at[chunk, dp], dst.at[chunk, dp], recv_sems.at[chunk]
+        ).start()
+        for x, y in FAR_FIRST:
+            peer = column[x] + line[y]
+            remote(
+                src.at[chunk, peer],
+                dst.at[chunk, dp],
+                send_sems.at[chunk],
+                recv_sems.at[chunk],
+                (peer, sq),
+            ).start()
 
     def pack_pair(block, array, pair):
         for half in range(2):
@@ -192,6 +189,7 @@
         return carry
 
     lax.fori_loop(0, DP // 2, norm_body, 0)
+    send(G, 0)
     gate_store = pltpu.make_async_copy(gstage, gate_grad, store_sem.at[0])
     gate_store.start()
     pack(V, 5)
@@ -382,11 +380,11 @@
         scatter_dp(osend, orecv, osend_sem, orecv_sem, chunk)
 
     gather_rows(Q, 0)
-    send(G, 0)
+    send(V, 0)
     gather_rows(K, 0)
-    send(V, 0)
+    send(Q, 1)
     gather_rows(G, 0)
-    send(Q, 1)
+    send(K, 1)
 
     @pl.when(core == 0)
     def _():
@@ -395,7 +393,7 @@
         lax.fori_loop(0, 1, scores_strip, 0)
 
     gather_rows(V, 0)
-    send(K, 1)
+    send(G, 1)
 
     @pl.when(core == 0)
     def _():
@@ -405,7 +403,7 @@
         send_grads(DV)
 
     gather_rows(Q, 1)
-    send(G, 1)
+    send(V, 1)
 
     @pl.when(core == 0)
     def _():
@@ -413,7 +411,6 @@
         lax.fori_loop(0, TILES, score_grad_strip, 0)
 
     gather_rows(K, 1)
-    send(V, 1)
 
     @pl.when(core == 0)
     def _():
@@ -432,11 +429,15 @@
 
     gather_rows(V, 1)
     return_rows(DV, 0)
+
+    @pl.when(core == 1)
+    def _():
+        lax.fori_loop(1, TILES, scores_strip, 0)
+
     return_rows(DK, 0)
 
     @pl.when(core == 1)
     def _():
-        lax.fori_loop(1, TILES, scores_strip, 0)
         history(G)
         later_sum(DV, G, 1.0)
         send_grads(DV)

time: 84.9 us -> 84.2 us (level)
  no operation moved by 1% of the time
where the time goes in v5:
time: 84.2 us; the launch traced here: 84 us
  Pallas kernels  82.6 us (98%)
  between operations  1.45 us (2%)
    pallas_call x1, Pallas kernels, local(): pl.pallas_call(kernel, out_shape=(arrived, gate_out), in_specs=[hbm] * 6...  79.7 us
    pallas_call x1, Pallas kernels, local(): pl.pallas_call(unpack, out_shape=(out,) * 4, in_specs=[hbm] * 2, out_spec...  2.85 us

profile of v5, /device:TPU:0, one launch (start us, length us, event | category | flops | bytes accessed | tf_op | source)
XLA Modules:
  0.0 84.0 jit_solution(50476044370867301)
XLA Ops:
  1.3 79.7 %shard_map.120 = (bf16[6,16,48,256]{3,2,1,0:T(8,128)(2,1)}, bf16[384,1024]{1,0:T(8,128)(2,1)}) custom-call(bf16[1,1,384,1024]{3,2,1,0:T(8,128)(2,1)} %queries.1, bf16[1,1,384,1024]{3,2,1,0:T(8,128)(2,1)} %keys.1, bf16[1,1,384,1024]{3,2,1,0:T(8,128)(2,1)} %values.1, bf16[1,1,384,1024]{3,2,1,0:T(8,128)(2,1)} %gates.1, bf16[1,1,384,1024]{3,2,1,0:T(8,128)(2,1)} %attended.1, ...), custom_call_target="tpu_custom_call" | custom-call | tf_op jit(solution)/shard_map/pallas_call | solution.py:521
  81.0 2.9 %shard_map.121 = (bf16[1,1,384,1024]{3,2,1,0:T(8,128)(2,1)}, bf16[1,1,384,1024]{3,2,1,0:T(8,128)(2,1)}, bf16[1,1,384,1024]{3,2,1,0:T(8,128)(2,1)}, bf16[1,1,384,1024]{3,2,1,0:T(8,128)(2,1)}) custom-call(bf16[6,16,48,256]{3,2,1,0:T(8,128)(2,1)} %get-tuple-element.6.moved, bf16[384,1024]{1,0:T(8,128)(2,1)} %get-tuple-element.7.gate_in), custom_call_target="tpu_custom_call" | custom-call | tf_op jit(solution)/shard_map/pallas_call | solution.py:557

commit v6 on v5

--- a/solution.py
+++ b/solution.py
@@ -135,8 +135,8 @@
                 (peer, sq),
             ).start()
 
-    def pack_pair(block, array, pair):
-        for half in range(2):
+    def pack_pair(block, array, pair, halves=(0, 1)):
+        for half in halves:
             for side in range(2):
                 part = block[side * SLOT : (side + 1) * SLOT]
                 at = half * HALF
@@ -145,12 +145,11 @@
                 )
                 dsend[2 * array + half, 2 * pair + side] = message.astype(BF16)
 
-    def pack(array, slot):
-        loads[slot].wait()
-
+    def pack(array, slot, halves=(0, 1)):
         def body(pair, carry):
             at = pl.multiple_of(pair * PACK, PACK)
-            pack_pair(stage[slot, pl.ds(at, PACK), :].astype(F32), array, pair)
+            block = stage[slot, pl.ds(at, PACK), :].astype(F32)
+            pack_pair(block, array, pair, halves)
             return carry
 
         lax.fori_loop(0, DP // 2, body, 0)
@@ -158,11 +157,15 @@
     def send(array, half):
         scatter_dp(dsend, drecv, dsend_sem, drecv_sem, 2 * array + half)
 
-    pack(Q, 0)
+    loads[0].wait()
+    pack(Q, 0, (0,))
     pl.semaphore_wait(barrier, DP - 1 + SEQ - 1)
     send(Q, 0)
-    pack(K, 1)
+    loads[1].wait()
+    pack(K, 1, (0,))
     send(K, 0)
+    pack(Q, 0, (1,))
+    pack(K, 1, (1,))
 
     for i in (2, 3, 4):
         loads[i].wait()
@@ -192,6 +195,7 @@
     send(G, 0)
     gate_store = pltpu.make_async_copy(gstage, gate_grad, store_sem.at[0])
     gate_store.start()
+    loads[5].wait()
     pack(V, 5)
 
     lane768 = lax.broadcasted_iota(jnp.int32, (1, DP * PACK), 1)
@@ -441,13 +445,13 @@
         history(G)
         later_sum(DV, G, 1.0)
         send_grads(DV)
-
-    return_rows(DQ, 0)
-
-    @pl.when(core == 1)
-    def _():
         history(V)
         lax.fori_loop(0, TILES, score_grad_strip, 0)
+
+    return_rows(DQ, 0)
+
+    @pl.when(core == 1)
+    def _():
         later_sum(DK, Q, SCALE)
         send_grads(DK)
         query_sum()

time: 84.2 us -> 84.2 us (level)
  no operation moved by 1% of the time
where the time goes in v6:
time: 84.2 us; the launch traced here: 84 us
  Pallas kernels  82.6 us (98%)
  between operations  1.45 us (2%)
    pallas_call x1, Pallas kernels, local(): pl.pallas_call(kernel, out_shape=(arrived, gate_out), in_specs=[hbm] * 6...  79.7 us
    pallas_call x1, Pallas kernels, local(): pl.pallas_call(unpack, out_shape=(out,) * 4, in_specs=[hbm] * 2, out_spec...  2.85 us

profile of v6, /device:TPU:0, one launch (start us, length us, event | category | flops | bytes accessed | tf_op | source)
XLA Modules:
  0.0 84.0 jit_solution(3048986236441638720)
XLA Ops:
  1.3 79.7 %shard_map.120 = (bf16[6,16,48,256]{3,2,1,0:T(8,128)(2,1)}, bf16[384,1024]{1,0:T(8,128)(2,1)}) custom-call(bf16[1,1,384,1024]{3,2,1,0:T(8,128)(2,1)} %queries.1, bf16[1,1,384,1024]{3,2,1,0:T(8,128)(2,1)} %keys.1, bf16[1,1,384,1024]{3,2,1,0:T(8,128)(2,1)} %values.1, bf16[1,1,384,1024]{3,2,1,0:T(8,128)(2,1)} %gates.1, bf16[1,1,384,1024]{3,2,1,0:T(8,128)(2,1)} %attended.1, ...), custom_call_target="tpu_custom_call" | custom-call | tf_op jit(solution)/shard_map/pallas_call | solution.py:525
  81.0 2.9 %shard_map.121 = (bf16[1,1,384,1024]{3,2,1,0:T(8,128)(2,1)}, bf16[1,1,384,1024]{3,2,1,0:T(8,128)(2,1)}, bf16[1,1,384,1024]{3,2,1,0:T(8,128)(2,1)}, bf16[1,1,384,1024]{3,2,1,0:T(8,128)(2,1)}) custom-call(bf16[6,16,48,256]{3,2,1,0:T(8,128)(2,1)} %get-tuple-element.6.moved, bf16[384,1024]{1,0:T(8,128)(2,1)} %get-tuple-element.7.gate_in), custom_call_target="tpu_custom_call" | custom-call | tf_op jit(solution)/shard_map/pallas_call | solution.py:561
